TPU v7x, 128 devices: a whole 4x4x4 slice. The times are simulated.
128 devices in a mesh: row: 16 (over x, z_lo, core), col: 8 (over y, z_hi).
Axes of the slice: x: 4, y: 4, z: 4 (z_hi: 2, z_lo: 2; z = z_hi * 2 + z_lo), core: 2. Of those that a mesh axis runs over, the one named last changes fastest.
Arguments:
- volume: bfloat16 [512, 8192], P('row', 'col'), may hold values from -6 to 6
- filters: bfloat16 [27, 512, 512], P(None, 'row', 'col'), may hold values from -0.0546875 to 0.0546875
- bias: bfloat16 [512], P('col'), may hold values from -3 to 3
- cotangent: bfloat16 [512, 8192], P('row', 'col'), may hold values from -6 to 6
Outputs:
- output: bfloat16 [512, 8192], P('row', 'col')
- data_grad: bfloat16 [512, 8192], P('row', 'col')
- weight_grad: float32 [27, 512, 512], P(None, 'row', 'col')
- bias_grad: float32 [512], P('row')
All inputs are finite; a program needn't handle non-finite values.
Results may differ from a plain program's by a relative error of at most 0.0075.
Values may be sent and summed in bfloat16 or wider, within the bound.
A program may use at most 192 MiB of HBM per device.

v0:
```python
import math

import jax
import jax.numpy as jnp
from jax import lax
from jax.sharding import PartitionSpec as P

F = 512
S = 32


def with_halo(block, sides, width):
    for axis, dim in sides:
        count = lax.axis_size(axis)
        forward = [(i, i + 1) for i in range(count - 1)]
        backward = [(target, source) for source, target in forward]
        low = lax.ppermute(
            lax.slice_in_dim(block, block.shape[dim] - width, None, axis=dim), axis, forward
        )
        high = lax.ppermute(lax.slice_in_dim(block, 0, width, axis=dim), axis, backward)
        block = jnp.concatenate([low, block, high], axis=dim)
    return block


def silu_slope(value):
    logistic = jax.nn.sigmoid(value)
    return logistic * (1.0 + value * (1.0 - logistic))


def pad_planes(flat, planes):
    shaped = flat.reshape(flat.shape[0], planes + 2, S, S)
    return jnp.pad(shaped, ((0, 0), (0, 0), (1, 1), (1, 1)))


def tap_view(padded, tap_index, planes, flipped):
    depth = tap_index // 9
    height = tap_index // 3 % 3
    across = tap_index % 3
    if flipped:
        depth, height, across = (2 - depth, 2 - height, 2 - across)
    piece = padded[:, depth : depth + planes, height : height + S, across : across + S]
    return piece.reshape(padded.shape[0], planes * S * S)


def conv_rows(weights, padded, planes):
    total = jnp.zeros((weights.shape[2], planes * S * S), jnp.float32)
    for tap_index in range(27):
        view = tap_view(padded, tap_index, planes, False)
        total = total + lax.dot_general(
            weights[tap_index], view, (((0,), (0,)), ((), ())), preferred_element_type=jnp.float32
        )
    return total


def on_device(volume, filters, bias, cotangent):
    col_count = lax.axis_size("col")
    row_count = lax.axis_size("row")
    planes = volume.shape[1] // (S * S)
    norm_factor = 1.0 / math.sqrt(planes * col_count * S * S)
    filter_share = F // row_count
    all_filters, all_bias = (
        lax.all_gather(filters, "col", axis=2, tiled=True),
        lax.all_gather(bias, "col", axis=0, tiled=True),
    )
    first_filter = lax.axis_index("row") * filter_share
    own_bias = lax.dynamic_slice_in_dim(all_bias, first_filter, filter_share, 0).astype(jnp.float32)
    rimmed = with_halo(volume, (("col", 1),), S * S)
    own_padded = pad_planes(rimmed, planes)
    summed = lax.psum_scatter(
        conv_rows(all_filters, own_padded, planes), "row", scatter_dimension=0, tiled=True
    )
    sectioned = summed + own_bias[:, None]
    output = jax.nn.silu(sectioned).astype(jnp.bfloat16)
    slope_grad = (cotangent.astype(jnp.float32) * silu_slope(sectioned)).astype(jnp.bfloat16)
    bias_local = jnp.sum(slope_grad.astype(jnp.float32), axis=1)
    bias_grad = lax.psum(bias_local, "col") * norm_factor
    plain_grad = lax.all_gather(slope_grad, "row", axis=0, tiled=True)
    grad_all = with_halo(plain_grad, (("col", 1),), S * S)
    center = grad_all[:, S * S : S * S + planes * S * S]
    weight_terms = []
    for tap_index in range(27):
        view = tap_view(own_padded, tap_index, planes, False)
        weight_terms.append(
            lax.dot_general(
                view, center, (((1,), (1,)), ((), ())), preferred_element_type=jnp.float32
            )
        )
    weight_stack = jnp.stack(weight_terms)
    weight_grad = (
        lax.psum_scatter(weight_stack, "col", scatter_dimension=2, tiled=True) * norm_factor
    )
    grad_padded = pad_planes(grad_all, planes)
    data_sum = jnp.zeros((volume.shape[0], planes * S * S), jnp.float32)
    for tap_index in range(27):
        view = tap_view(grad_padded, tap_index, planes, True)
        data_sum = data_sum + jnp.dot(
            all_filters[tap_index], view, preferred_element_type=jnp.float32
        )
    return (output, data_sum.astype(jnp.bfloat16), weight_grad, bias_grad)


def solution(mesh):
    placed = (P("row", "col"), P(None, "row", "col"), P("col"), P("row", "col"))
    return jax.shard_map(
        on_device,
        mesh=mesh,
        in_specs=placed,
        out_specs=(P("row", "col"), P("row", "col"), P(None, "row", "col"), P("row")),
        check_vma=False,
    )
```

profile of v0, /device:TPU:1, one launch (start us, length us, event | category | flops | bytes accessed | tf_op | source)
XLA Modules:
  0.0 480.7 jit_solution(7459935159036338463)
XLA Ops:
  7.2 6.3 %collective-permute-start = (bf16[32,1024]{1,0:T(8,128)(2,1)}, bf16[32,1024]{1,0:T(8,128)(2,1)S(1)}, u32[]{:S(2)}, u32[]{:S(2)}) collective-permute-start(bf16[32,1024]{1,0:T(8,128)(2,1)} %param.4), channel_id=1, source_target_pairs={{0,1},{1,2},{2,3},{3,4},{4,5},{5,6},{6,7},{8,9},{9,10},{10,11},{11... | collective-permute-start | bytes 196616 | tf_op jit(solution)/shard_map/ppermute | solution.py:17
  14.9 1.7 copy.48
  16.6 87.6 %all_gather.9 = bf16[27,32,512]{1,0,2:T(8,128)(2,1)S(1)} all-gather(bf16[27,32,64]{1,0,2:T(8,128)(2,1)S(1)} %copy.48), channel_id=1, replica_groups=mesh['row'=16,'col'=8] {'col'}, dimensions={2}, use_global_device_ids=true | all-gather | bytes 995328 | tf_op jit(solution)/shard_map/all_gather | solution.py:62
  104.2 4.9 %fusion.120 = (bf16[1,32,512]{1,0,2:T(2,128)(2,1)S(1)}, bf16[1,32,512]{1,0,2:T(2,128)(2,1)S(1)}, bf16[1,32,512]{1,0,2:T(2,128)(2,1)S(1)}, bf16[1,32,512]{1,0,2:T...) fusion(bf16[27,32,512]{1,0,2:T(8,128)(2,1)S(1)} %all_gather.9), kind=kLoop, calls=%fused_computation.240 | loop fusion | bytes 1245184 | tf_op jit(solution)/shard_map/slice | solution.py:50
  109.1 2.9 fusion.121
  111.9 1.7 copy.104
  123.5 1.7 copy.96
  131.5 1.7 copy.87
  133.2 1.7 copy.86
  134.9 1.7 copy.85
  144.9 3.5 pad_slice_fusion.24
  151.5 1.9 reshape.223
  153.4 1.9 reshape.222
  155.3 1.9 reshape.221
  157.1 1.9 reshape.220
  159.0 1.9 reshape.219
  160.9 1.9 reshape.217
  163.6 1.9 reshape.215
  165.5 1.9 reshape.214
  167.4 1.9 reshape.213
  169.2 1.9 reshape.210
  171.1 1.9 reshape.208
  177.5 1.8 fusion.57
  179.2 1.8 fusion.60
  181.0 1.8 fusion.63
  182.8 1.8 fusion.66
  184.7 1.8 fusion.69
  186.5 1.8 fusion.72
  188.3 1.8 fusion.75
  190.1 1.8 fusion.81
  192.0 1.8 fusion.84
  193.8 1.8 fusion.87
  195.6 1.8 fusion.90
  197.4 1.8 fusion.93
  199.2 1.8 fusion.102
  200.9 1.8 fusion.108
  202.7 1.8 fusion.111
  204.5 1.8 fusion.115
  206.3 1.8 fusion.42
  208.1 1.8 fusion.45
  209.9 1.8 fusion.48
  211.7 1.7 fusion.51
  213.4 1.8 fusion.54
  215.2 1.8 fusion.78
  217.0 1.8 fusion.96
  218.8 1.8 fusion.99
  220.6 1.8 fusion.105
  222.4 1.8 fusion.118
  224.2 17.9 %bitcast_add_fusion = f32[512,1024]{0,1:T(8,128)S(1)} fusion(f32[1024,512]{1,0:T(8,128)} %fusion.42, f32[1024,512]{1,0:T(8,128)} %fusion.45, f32[1024,512]{1,0:T(8,128)} %fusion.48, f32[1024,512]{1,0:T(8,128)} %fusion.51, f32[1024,512]{1,0:T(8,128)} %fusion.54, f32[1024,512]{1,0:T(8,128)} %fusion.57, f32[1024,512]{1,0:T(8,128)} %fusion.60, ...), kind=kOutput, calls=%fused_computation.25 | convolution fusion | flops 47185920 | bytes 56721408 | tf_op jit(solution)/shard_map/dot_general | solution.py:49
  242.1 1.8 copy.80
  246.1 16.0 %all-reduce.2 = bf16[512]{0:T(512)(128)(2,1)S(1)} all-reduce(bf16[512]{0:T(512)(128)(2,1)S(1)} %dynamic-update-slice), channel_id=1, replica_groups=mesh['row'=16,'col'=8] {'col'}, use_global_device_ids=true, to_apply=%add.2 | all-reduce | flops 512 | bytes 2048
  262.2 41.7 %reduce-scatter.7.cloned.1.call-done = f32[32,1024]{1,0:T(8,128)} async-done(((f32[512,1024]{1,0:T(8,128)}), f32[32,1024]{1,0:T(8,128)}) %reduce-scatter.7.cloned.1.call-update) | async-done | bytes 131088 | tf_op jit(solution)/shard_map/reduce_scatter | solution.py:69
  303.9 1.8 convert_reduce_fusion
  305.8 20.7 %psum.7 = f32[32]{0:T(128)S(1)} all-reduce(f32[32]{0:T(128)S(1)} %get-tuple-element.16), channel_id=1, replica_groups=mesh['row'=16,'col'=8] {'col'}, use_global_device_ids=true, to_apply=%region_3.4 | all-reduce | flops 32 | bytes 256 | tf_op jit(solution)/shard_map/psum | solution.py:76
  327.0 14.0 %all-gather.2.cloned.1.call-done = bf16[512,1024]{1,0:T(8,128)(2,1)} async-done(((bf16[32,1024]{1,0:T(8,128)(2,1)}), bf16[512,1024]{1,0:T(8,128)(2,1)}) %all-gather.2.cloned.1.call-update) | async-done | bytes 1048592 | tf_op jit(solution)/shard_map/all_gather | solution.py:77
  342.7 4.7 collective-permute-start.2
  348.9 1.9 fusion.38
  350.7 1.9 fusion.37
  352.7 1.9 fusion.36
  379.6 8.6 %copy.82 = f32[27,32,512]{1,0,2:T(8,128)} copy(f32[27,32,512]{2,1,0:T(8,128)} %fusion.12) | data formatting | bytes 3538944
  388.3 7.0 %reshape.267 = f32[512,864]{1,0:T(8,128)} reshape(f32[512,27,32]{2,1,0:T(8,128)} %bitcast.523) | data formatting | bytes 3538944
  396.6 8.0 %pad_slice_fusion.1 = (bf16[512,1,32,32]{0,3,2,1:T(8,128)(2,1)S(1)}, bf16[512,1,32,32]{0,3,2,1:T(8,128)(2,1)}, bf16[512,1,32,32]{0,3,2,1:T(8,128)(2,1)}, bf16[51...) fusion(bf16[512,3,32,32]{0,3,2,1:T(8,128)(2,1)S(1)} %bitcast.521), kind=kLoop, calls=%fused_computation.1 | loop fusion | bytes 23068672 | tf_op jit(solution)/shard_map/slice | solution.py:41
  404.7 3.2 pad_slice_fusion.3
  420.7 50.5 %reduce-scatter.9.cloned.1.call-done = f32[64,864]{1,0:T(8,128)} async-done(((f32[512,864]{1,0:T(8,128)}), f32[64,864]{1,0:T(8,128)}) %reduce-scatter.9.cloned.1.call-update) | async-done | bytes 221200
  (350 shorter events, 81.2 us)
Async XLA Ops:
  7.2 296.8 %reduce-scatter.7.cloned.1.call-start = ((), (), s32[]{:S(2)}) async-start(), calls=%async_computation.3 | async-start | bytes 2228224 | tf_op jit(solution)/shard_map/reduce_scatter | solution.py:69
  7.2 137.1 %collective-permute-start = (bf16[32,1024]{1,0:T(8,128)(2,1)}, bf16[32,1024]{1,0:T(8,128)(2,1)S(1)}, u32[]{:S(2)}, u32[]{:S(2)}) collective-permute-start(bf16[32,1024]{1,0:T(8,128)(2,1)} %param.4), channel_id=1, source_target_pairs={{0,1},{1,2},{2,3},{3,4},{4,5},{5,6},{6,7},{8,9},{9,10},{10,11},{11... | collective-permute-start | bytes 196616 | tf_op jit(solution)/shard_map/ppermute | solution.py:17
  13.6 130.7 %collective-permute-start.1 = (bf16[32,1024]{1,0:T(8,128)(2,1)}, bf16[32,1024]{1,0:T(8,128)(2,1)S(1)}, u32[]{:S(2)}, u32[]{:S(2)}) collective-permute-start(bf16[32,1024]{1,0:T(8,128)(2,1)} %param.4), channel_id=1, source_target_pairs={{1,0},{2,1},{3,2},{4,3},{5,4},{6,5},{7,6},{9,8},{10,9},{11,10},{12... | collective-permute-start | bytes 196616 | tf_op jit(solution)/shard_map/ppermute | solution.py:20
  131.5 12.8 %copy-start.115 = (bf16[32,1024]{1,0:T(8,128)(2,1)S(1)}, bf16[32,1024]{1,0:T(8,128)(2,1)}, u32[]{:S(2)}) copy-start(bf16[32,1024]{1,0:T(8,128)(2,1)} %param.4) | copy-start | bytes 196612
  148.9 13.8 %copy-start.16 = (bf16[32,1,32,32]{3,2,1,0:T(8,128)(2,1)S(1)}, bf16[32,1,32,32]{3,2,1,0:T(8,128)(2,1)}, u32[]{:S(2)}) copy-start(bf16[32,1,32,32]{3,2,1,0:T(8,128)(2,1)} %get-tuple-element.82) | copy-start | bytes 196612
  150.2 22.7 %copy-start.15 = (bf16[32,1,32,32]{3,2,1,0:T(8,128)(2,1)S(1)}, bf16[32,1,32,32]{3,2,1,0:T(8,128)(2,1)}, u32[]{:S(2)}) copy-start(bf16[32,1,32,32]{3,2,1,0:T(8,128)(2,1)} %get-tuple-element.74) | copy-start | bytes 196612
  151.5 22.3 %copy-start.14 = (bf16[32,1,32,32]{3,2,1,0:T(8,128)(2,1)S(1)}, bf16[32,1,32,32]{3,2,1,0:T(8,128)(2,1)}, u32[]{:S(2)}) copy-start(bf16[32,1,32,32]{3,2,1,0:T(8,128)(2,1)} %get-tuple-element.73) | copy-start | bytes 196612
  163.6 12.2 %copy-start.13 = (bf16[32,1,32,32]{3,2,1,0:T(8,128)(2,1)S(1)}, bf16[32,1,32,32]{3,2,1,0:T(8,128)(2,1)}, u32[]{:S(2)}) copy-start(bf16[32,1,32,32]{3,2,1,0:T(8,128)(2,1)} %get-tuple-element.78) | copy-start | bytes 196612
  174.1 30.4 %copy-start.52 = (bf16[32,1024]{1,0:T(8,128)(2,1)}, bf16[32,1024]{1,0:T(8,128)(2,1)S(1)}, u32[]{:S(2)}) copy-start(bf16[32,1024]{1,0:T(8,128)(2,1)S(1)} %reshape.206) | copy-start | bytes 196612
  174.4 31.9 %copy-start.19 = (bf16[32,1024]{1,0:T(8,128)(2,1)}, bf16[32,1024]{1,0:T(8,128)(2,1)S(1)}, u32[]{:S(2)}) copy-start(bf16[32,1024]{1,0:T(8,128)(2,1)S(1)} %reshape.230) | copy-start | bytes 196612
  174.7 33.4 %copy-start.22 = (bf16[32,1024]{1,0:T(8,128)(2,1)}, bf16[32,1024]{1,0:T(8,128)(2,1)S(1)}, u32[]{:S(2)}) copy-start(bf16[32,1024]{1,0:T(8,128)(2,1)S(1)} %reshape.229) | copy-start | bytes 196612
  174.9 34.9 %copy-start.25 = (bf16[32,1024]{1,0:T(8,128)(2,1)}, bf16[32,1024]{1,0:T(8,128)(2,1)S(1)}, u32[]{:S(2)}) copy-start(bf16[32,1024]{1,0:T(8,128)(2,1)S(1)} %reshape.228) | copy-start | bytes 196612
  175.2 36.4 %copy-start.29 = (bf16[32,1024]{1,0:T(8,128)(2,1)}, bf16[32,1024]{1,0:T(8,128)(2,1)S(1)}, u32[]{:S(2)}) copy-start(bf16[32,1024]{1,0:T(8,128)(2,1)S(1)} %reshape.227) | copy-start | bytes 196612
  175.5 37.9 %copy-start.31 = (bf16[32,1024]{1,0:T(8,128)(2,1)}, bf16[32,1024]{1,0:T(8,128)(2,1)S(1)}, u32[]{:S(2)}) copy-start(bf16[32,1024]{1,0:T(8,128)(2,1)S(1)} %reshape.226) | copy-start | bytes 196612
  175.5 3.7 copy-start.60
  175.8 39.4 %copy-start.43 = (bf16[32,1024]{1,0:T(8,128)(2,1)}, bf16[32,1024]{1,0:T(8,128)(2,1)S(1)}, u32[]{:S(2)}) copy-start(bf16[32,1024]{1,0:T(8,128)(2,1)S(1)} %reshape.218) | copy-start | bytes 196612
  176.1 40.9 %copy-start.50 = (bf16[32,1024]{1,0:T(8,128)(2,1)}, bf16[32,1024]{1,0:T(8,128)(2,1)S(1)}, u32[]{:S(2)}) copy-start(bf16[32,1024]{1,0:T(8,128)(2,1)S(1)} %reshape.212) | copy-start | bytes 196612
  176.4 42.4 %copy-start.53 = (bf16[32,1024]{1,0:T(8,128)(2,1)}, bf16[32,1024]{1,0:T(8,128)(2,1)S(1)}, u32[]{:S(2)}) copy-start(bf16[32,1024]{1,0:T(8,128)(2,1)S(1)} %reshape.211) | copy-start | bytes 196612
  176.7 47.5 %copy-start.58 = (bf16[32,1024]{1,0:T(8,128)(2,1)}, bf16[32,1024]{1,0:T(8,128)(2,1)S(1)}, u32[]{:S(2)}) copy-start(bf16[32,1024]{1,0:T(8,128)(2,1)S(1)} %reshape.231) | copy-start | bytes 196612
  177.0 43.6 %copy-start.55 = (bf16[32,1024]{1,0:T(8,128)(2,1)}, bf16[32,1024]{1,0:T(8,128)(2,1)S(1)}, u32[]{:S(2)}) copy-start(bf16[32,1024]{1,0:T(8,128)(2,1)S(1)} %reshape.209) | copy-start | bytes 196612
  177.4 45.0 %copy-start.57 = (bf16[32,1024]{1,0:T(8,128)(2,1)}, bf16[32,1024]{1,0:T(8,128)(2,1)S(1)}, u32[]{:S(2)}) copy-start(bf16[32,1024]{1,0:T(8,128)(2,1)S(1)} %reshape.205) | copy-start | bytes 196612
  179.2 3.6 copy-start.18
  179.2 3.6 copy-start.62
  181.0 3.7 copy-start.21
  181.0 3.7 copy-start.82
  182.8 3.6 copy-start.24
  182.8 3.6 copy-start.84
  186.5 3.7 copy-start.33
  186.5 3.7 copy-start.88
  188.3 3.7 copy-start.35
  188.3 3.7 copy-start.90
  190.1 3.6 copy-start.37
  190.1 3.6 copy-start.92
  193.8 3.6 copy-start.41
  193.8 3.6 copy-start.98
  206.3 3.6 copy-start.66
  218.8 3.6 copy-start.112
  220.6 3.6 copy-start.74
  243.9 60.0 %copy-start.114 = (bf16[32,1024]{1,0:T(8,128)(2,1)S(1)}, bf16[32,1024]{1,0:T(8,128)(2,1)}, u32[]{:S(2)}) copy-start(bf16[32,1024]{1,0:T(8,128)(2,1)} %param.7) | copy-start | bytes 196612
  244.0 97.1 %all-gather.2.cloned.1.call-start = ((), (), s32[]{:S(2)}) async-start(), calls=%async_computation.2 | async-start | bytes 1114112 | tf_op jit(solution)/shard_map/all_gather | solution.py:77
  305.8 165.5 %reduce-scatter.9.cloned.1.call-start = ((), (), s32[]{:S(2)}) async-start(), calls=%async_computation.4 | async-start | bytes 2064384
  341.1 7.8 %copy-start = (bf16[512,1024]{1,0:T(8,128)(2,1)S(1)}, bf16[512,1024]{1,0:T(8,128)(2,1)}, u32[]{:S(2)}) copy-start(bf16[512,1024]{1,0:T(8,128)(2,1)} %all-gather.2.cloned.1.call-done) | copy-start | bytes 3145732
  342.6 11.9 %copy-start.48 = (bf16[32,1024]{1,0:T(8,128)(2,1)S(1)}, bf16[32,1024]{1,0:T(8,128)(2,1)}, u32[]{:S(2)}) copy-start(bf16[32,1024]{1,0:T(8,128)(2,1)} %reshape.208) | copy-start | bytes 196612
  342.7 13.0 %copy-start.56 = (bf16[32,1024]{1,0:T(8,128)(2,1)S(1)}, bf16[32,1024]{1,0:T(8,128)(2,1)}, u32[]{:S(2)}) copy-start(bf16[32,1024]{1,0:T(8,128)(2,1)} %copy-done.55) | copy-start | bytes 196612
  342.7 52.6 %collective-permute-start.2 = (bf16[512,1024]{0,1:T(8,128)(2,1)S(1)}, bf16[512,1024]{0,1:T(8,128)(2,1)S(1)}, u32[]{:S(2)}, u32[]{:S(2)}) collective-permute-start(bf16[512,1024]{0,1:T(8,128)(2,1)S(1)} %copy.77), channel_id=1, source_target_pairs={{0,1},{1,2},{2,3},{3,4},{4,5},{5,6},{6,7},{8,9},{9,10},{10,11},{11... | collective-permute-start | bytes 3145736 | tf_op jit(solution)/shard_map/ppermute | solution.py:17
  347.3 47.9 %collective-permute-start.3 = (bf16[512,1024]{0,1:T(8,128)(2,1)S(1)}, bf16[512,1024]{0,1:T(8,128)(2,1)}, u32[]{:S(2)}, u32[]{:S(2)}) collective-permute-start(bf16[512,1024]{0,1:T(8,128)(2,1)S(1)} %copy.77), channel_id=1, source_target_pairs={{1,0},{2,1},{3,2},{4,3},{5,4},{6,5},{7,6},{9,8},{10,9},{11,10},{12... | collective-permute-start | bytes 3145736 | tf_op jit(solution)/shard_map/ppermute | solution.py:20
  350.7 5.9 %copy-start.46 = (bf16[32,1024]{1,0:T(8,128)(2,1)S(1)}, bf16[32,1024]{1,0:T(8,128)(2,1)}, u32[]{:S(2)}) copy-start(bf16[32,1024]{1,0:T(8,128)(2,1)} %reshape.210) | copy-start | bytes 196612
  352.7 5.1 %copy-start.54 = (bf16[32,1024]{1,0:T(8,128)(2,1)S(1)}, bf16[32,1024]{1,0:T(8,128)(2,1)}, u32[]{:S(2)}) copy-start(bf16[32,1024]{1,0:T(8,128)(2,1)} %copy-done.53) | copy-start | bytes 196612
  354.6 4.2 copy-start.51
  355.6 4.2 copy-start.42
  356.7 4.2 copy-start.40
  357.7 4.2 copy-start.38
  358.8 4.2 copy-start.36
  359.8 4.2 copy-start.34
  360.9 4.2 copy-start.44
  361.9 4.2 copy-start.28
  369.2 4.2 copy-start.32
  370.3 4.2 copy-start.30
  371.3 4.2 copy-start.26
  372.3 4.2 copy-start.23
  373.4 4.2 copy-start.20
  374.4 4.2 copy-start.59
  404.6 3.7 copy-start.11
  404.6 3.7 copy-start.73
  (61 other events, 135.2 us)
Sparse Core Ops, SparseCore 0:
  244.1 59.7 reduce-scatter.6
  306.2 34.8 all-gather.1
  395.4 75.8 reduce-scatter.8
where the time goes:
time: 486 us; the launch traced here: 481 us
  blocking collectives  124 us (26%)
  local copies, waits for them, and re-layouts  109 us (22%)
  matrix products  107 us (22%)
  waiting for transfers between devices  106 us (22%)
  between operations  15.7 us (3%)
  starting transfers between devices  13.9 us (3%)
    all_gather x1, blocking collectives, on_device(): lax.all_gather(filters, 'col', axis=2, tiled=True)  87.6 us
    dot_general x27, matrix products, conv_rows(): lax.dot_general(weights[tap_index], view, (((0,), (0,)), ((), ())), prefe...  64.4 us
    unnamed x272, local copies, waits for them, and re-layouts  55.8 us
    unnamed x4, waiting for transfers between devices  50.6 us
    reduce_scatter x1, waiting for transfers between devices, on_device(): lax.psum_scatter(conv_rows(all_filters, own_padded, planes), 'row', scatt...  41.7 us
    dot_general x27, matrix products, on_device(): lax.dot_general(view, center, (((1,), (1,)), ((), ())), preferred_element...  30.7 us
    reshape x27, local copies, waits for them, and re-layouts, tap_view(): return piece.reshape(padded.shape[0], planes * S * S)  28.3 us
    psum x1, blocking collectives, on_device(): bias_grad = lax.psum(bias_local, 'col') * norm_factor  20.7 us
  transfers between devices with their start and end apart: 7, of which 3 were waited for; matrix products, arithmetic and copies ran while one was open for 24% of the time, Pallas kernels for 0%

commit v1 on v0

v1 whole, which is shorter than its diff:
```python
import functools
import math

import jax
import jax.numpy as jnp
from jax import lax
from jax.experimental import pallas as pl
from jax.experimental.pallas import tpu as pltpu
from jax.sharding import PartitionSpec as P

S = 32
VOX = S * S
CH = 32
TAPS = 27
DEPTH = TAPS * CH
PADDED = 896
MESH = pl.DeviceIdType.MESH
BF16 = jnp.bfloat16
F32 = jnp.float32


def positions():
    lane = lax.broadcasted_iota(jnp.int32, (CH, VOX), 1)
    return lane // S, lane % S


def inside(coord, step):
    moved = coord + step
    return (moved >= 0) & (moved < S)


def moved_view(value, y, x, dy, dx):
    offset = dy * S + dx
    if offset:
        value = pltpu.roll(value, (-offset) % VOX, 1)
    if dy or dx:
        keep = inside(y, dy) & inside(x, dx)
        value = jnp.where(keep, value, 0.0)
    return value


def kernel(
    nc, norm_factor,
    vol_ref, w_ref, bias_ref, cot_ref,
    out_ref, dgrad_ref, wgrad_ref, bgrad_ref,
    wpad, wt_own, wg, xin, xcol, ypart, yrecv, g, wgp, wgrecv, bsend, brecv, z, dsend, dacc, drecv,
    x_send, x_recv, w_send, w_recv, y_send, y_recv, g_send, g_recv, b_send, b_recv, wg_send, wg_recv, d_send, d_recv,
):
    row = lax.axis_index("row")
    col = lax.axis_index("col")
    q = row // 2
    k = row % 2
    sib = 2 * q + 1 - k
    up = (col + 1) % nc
    down = (col + nc - 1) % nc

    def rows(start, size=CH):
        return pl.ds(pl.multiple_of(start, CH), size)

    def send(src, dst, send_sem, recv_sem, to_row, to_col):
        copy = pltpu.make_async_remote_copy(
            src_ref=src, dst_ref=dst, send_sem=send_sem, recv_sem=recv_sem,
            device_id=(to_row, to_col), device_id_type=MESH,
        )
        copy.start()
        return copy

    barrier = pltpu.get_barrier_semaphore()
    for d in range(nc):
        for o in range(2):
            if d or o:
                pl.semaphore_signal(
                    barrier, inc=1, device_id=(sib if o else row, (col + d) % nc), device_id_type=MESH
                )
    for j in range(1, nc):
        pl.semaphore_signal(
            barrier, inc=1, device_id=(2 * ((q + j) % nc) + k, col), device_id_type=MESH
        )

    wpad[...] = jnp.zeros_like(wpad)
    wpad[0:DEPTH, 0 : 2 * CH] = w_ref[...].reshape(DEPTH, 2 * CH).astype(F32)
    wpad[DEPTH : DEPTH + 1, 0 : 2 * CH] = bias_ref[...].astype(F32)
    wt_own[...] = jnp.transpose(wpad[...])[0 : 2 * CH].astype(BF16)
    xin[1, rows(CH * k), :] = vol_ref[...]
    bsend[...] = jnp.zeros_like(bsend)

    pl.semaphore_wait(barrier, 3 * nc - 2)

    copies = []
    x_copies = {}
    for a, to_col in ((1, col), (0, up), (2, down)):
        for o in range(2):
            if a == 1 and o == 0:
                continue
            x_copies[a, o] = send(
                vol_ref, xin.at[a, rows(CH * k), :], x_send.at[a, o], x_recv.at[a, o],
                sib if o else row, to_col,
            )
    w_copies = {}
    for d in range(nc):
        for o in range(2):
            half = 1 - k if o else k
            if d == 0 and o == 0:
                wg[k, 0:CH, :] = wt_own[rows(CH * k), :]
                continue
            w_copies[d, o] = send(
                wt_own.at[rows(CH * half), :], wg.at[k, pl.ds(CH * d, CH), :],
                w_send.at[d, o], w_recv.at[d, o], sib if o else row, (col + d) % nc,
            )
    copies += list(x_copies.values()) + list(w_copies.values())

    y, x = positions()
    for h in range(2):
        xcol[h, DEPTH:PADDED, :] = jnp.zeros((PADDED - DEPTH, VOX), BF16)
    low_ok = (col > 0).astype(F32)
    high_ok = (col < nc - 1).astype(F32)
    for a in (1, 0, 2):
        for o in range(2):
            if (a, o) in x_copies:
                x_copies[a, o].wait_recv()
        for h in range(2):
            plane = xin[a, CH * h : CH * h + CH, :].astype(F32)
            if a == 0:
                plane = plane * low_ok
            if a == 2:
                plane = plane * high_ok
            for b in range(3):
                for c in range(3):
                    tap = 9 * a + 3 * b + c
                    xcol[h, CH * tap : CH * tap + CH, :] = moved_view(plane, y, x, b - 1, c - 1).astype(BF16)

    for copy in w_copies.values():
        copy.wait_recv()
    ypart[...] = (
        jnp.dot(wg[0], xcol[0], preferred_element_type=F32)
        + jnp.dot(wg[1], xcol[1], preferred_element_type=F32)
    ).astype(BF16)

    y_copies = []
    for j in range(1, nc):
        owner = (q + j) % nc
        y_copies.append(
            send(
                ypart.at[rows(CH * ((col - owner + nc) % nc)), :], yrecv.at[j],
                y_send.at[j], y_recv.at[j], 2 * owner + k, col,
            )
        )
    copies += y_copies
    slot = rows(CH * ((col - q + nc) % nc))
    sectioned = ypart[slot, :].astype(F32)
    tail = wg[0, slot, PADDED - 128 : PADDED].astype(F32)
    lane = lax.broadcasted_iota(jnp.int32, (CH, 128), 1)
    own_bias = jnp.sum(jnp.where(lane == DEPTH - (PADDED - 128), tail, 0.0), axis=1, keepdims=True)
    for j, copy in enumerate(y_copies):
        copy.wait_recv()
        sectioned = sectioned + yrecv[j + 1].astype(F32)
    sectioned = sectioned + own_bias
    s = 1.0 / (1.0 + jnp.exp(-sectioned))
    out_ref[...] = (sectioned * s).astype(BF16)
    g[slot, :] = (cot_ref[...].astype(F32) * (s * (1.0 + sectioned * (1.0 - s)))).astype(BF16)

    g_copies = []
    for j in range(1, nc):
        g_copies.append(
            send(
                g.at[slot, :], g.at[slot, :], g_send.at[j], g_recv.at[j], 2 * ((q + j) % nc) + k, col
            )
        )
    bias_part = lax.dot_general(
        jnp.ones((8, VOX), BF16), g[slot, :], (((1,), (1,)), ((), ())), preferred_element_type=F32
    )
    bsend[:, 0:CH] = bias_part
    b_copies = []
    for d in range(1, nc):
        b_copies.append(
            send(bsend, brecv.at[d], b_send.at[d], b_recv.at[d], row, (col + d) % nc)
        )
    copies += g_copies + b_copies

    for copy in g_copies:
        copy.wait_recv()
    for h in range(2):
        wgp[h] = lax.dot_general(
            g[...], xcol[h], (((1,), (1,)), ((), ())), preferred_element_type=F32
        ).astype(BF16)
    wg_copies = []
    for d in range(nc):
        for o in range(2):
            h = 1 - k if o else k
            if d == 0 and o == 0:
                wgrecv[0, rows(CH * k), :] = wgp[k, 0:CH, :]
                continue
            wg_copies.append(
                send(
                    wgp.at[h, pl.ds(CH * d, CH), :], wgrecv.at[d, rows(CH * k), :],
                    wg_send.at[d, o], wg_recv.at[d, o], sib if o else row, (col - d + nc) % nc,
                )
            )
    copies += wg_copies

    for h in range(2):
        z[...] = lax.dot_general(
            wg[h], g[...], (((0,), (0,)), ((), ())), preferred_element_type=F32
        )
        for a in range(3):
            total = jnp.zeros((CH, VOX), F32)
            for b in range(3):
                for c in range(3):
                    tap = 9 * a + 3 * b + c
                    total = total + moved_view(z[CH * tap : CH * tap + CH, :], y, x, 1 - b, 1 - c)
            dsend[a, CH * h : CH * h + CH, :] = total.astype(BF16)
            if a == 1:
                dacc[h] = total
    d_copies = []
    for o in range(2):
        mine = rows(CH * (1 - k if o else k))
        for a, to_col in ((1, col), (2, up), (0, down)):
            if a == 1 and o == 0:
                continue
            d_copies.append(
                send(
                    dsend.at[a, mine, :], drecv.at[a, o], d_send.at[a, o], d_recv.at[a, o],
                    sib if o else row, to_col,
                )
            )
    copies += d_copies

    for copy in b_copies:
        copy.wait_recv()
    bias_sum = bsend[...]
    for d in range(1, nc):
        bias_sum = bias_sum + brecv[d]
    bgrad_ref[...] = bias_sum[0:1, 0:CH] * norm_factor

    for copy in d_copies:
        copy.wait_recv()
    data_sum = dacc[k] + drecv[1, 1].astype(F32)
    data_sum = data_sum + low_ok * (drecv[2, 0].astype(F32) + drecv[2, 1].astype(F32))
    data_sum = data_sum + high_ok * (drecv[0, 0].astype(F32) + drecv[0, 1].astype(F32))
    dgrad_ref[...] = data_sum.astype(BF16)

    for copy in wg_copies:
        copy.wait_recv()
    total = wgrecv[0].astype(F32)
    for d in range(1, nc):
        total = total + wgrecv[d].astype(F32)
    total = jnp.transpose(total * norm_factor)
    wgrad_ref[...] = total[0:DEPTH].reshape(TAPS, CH, 2 * CH)

    for copy in copies:
        copy.wait_send()


def on_device(nc, volume, filters, bias, cotangent):
    chunk = CH * nc
    dma = pltpu.SemaphoreType.DMA
    vmem = pl.BlockSpec(memory_space=pltpu.VMEM)
    output, data_grad, weight_grad, bias_grad = pl.pallas_call(
        functools.partial(kernel, nc, 1.0 / math.sqrt(nc * VOX)),
        out_shape=(
            jax.ShapeDtypeStruct((CH, VOX), BF16),
            jax.ShapeDtypeStruct((CH, VOX), BF16),
            jax.ShapeDtypeStruct((TAPS, CH, 2 * CH), F32),
            jax.ShapeDtypeStruct((1, CH), F32),
        ),
        in_specs=[vmem] * 4,
        out_specs=(vmem,) * 4,
        scratch_shapes=[
            pltpu.VMEM((PADDED, 128), F32),
            pltpu.VMEM((2 * CH, PADDED), BF16),
            pltpu.VMEM((2, chunk, PADDED), BF16),
            pltpu.VMEM((3, 2 * CH, VOX), BF16),
            pltpu.VMEM((2, PADDED, VOX), BF16),
            pltpu.VMEM((chunk, VOX), BF16),
            pltpu.VMEM((nc, CH, VOX), BF16),
            pltpu.VMEM((chunk, VOX), BF16),
            pltpu.VMEM((2, chunk, PADDED), BF16),
            pltpu.VMEM((nc, 2 * CH, PADDED), BF16),
            pltpu.VMEM((8, 128), F32),
            pltpu.VMEM((nc, 8, 128), F32),
            pltpu.VMEM((PADDED, VOX), F32),
            pltpu.VMEM((3, 2 * CH, VOX), BF16),
            pltpu.VMEM((2, CH, VOX), F32),
            pltpu.VMEM((3, 2, CH, VOX), BF16),
            dma((3, 2)), dma((3, 2)),
            dma((nc, 2)), dma((nc, 2)),
            dma((nc,)), dma((nc,)),
            dma((nc,)), dma((nc,)),
            dma((nc,)), dma((nc,)),
            dma((nc, 2)), dma((nc, 2)),
            dma((3, 2)), dma((3, 2)),
        ],
        compiler_params=pltpu.CompilerParams(
            collective_id=0, has_side_effects=True, vmem_limit_bytes=48 * 1024 * 1024
        ),
    )(volume, filters, bias.reshape(1, 2 * CH), cotangent)
    return output, data_grad, weight_grad, bias_grad.reshape(CH)


def solution(mesh):
    placed = (P("row", "col"), P(None, "row", "col"), P("col"), P("row", "col"))
    return jax.shard_map(
        functools.partial(on_device, mesh.shape["col"]),
        mesh=mesh,
        in_specs=placed,
        out_specs=(P("row", "col"), P("row", "col"), P(None, "row", "col"), P("row")),
        check_vma=False,
    )
```

time: 486 us -> 70.8 us (0.15); the launches traced: 481 us -> 70.5 us
  blocking collectives: 124 us -> 0 us
  matrix products: 107 us -> 0 us
  waiting for transfers between devices: 106 us -> 0 us
  local copies, waits for them, and re-layouts: 109 us -> 5.8 us
  Pallas kernels: 0 us -> 64.1 us
  between operations: 15.7 us -> 0.65 us
  starting transfers between devices: 13.9 us -> 0 us
    dot_general x81 -> x0, matrix products: 107 us -> none  [the longest x27 64.4 us: conv_rows(): lax.dot_general(weights[tap_index], view, (((0,), (0,)), ((), ())), prefe...]
    all_gather x1 -> x0, blocking collectives: 87.6 us -> none  [on_device(): lax.all_gather(filters, 'col', axis=2, tiled=True)]
    pallas_call x0 -> x1, Pallas kernels: none -> 64.1 us  [on_device(): pl.pallas_call(functools.partial(kernel, nc, 1.0 / math.sqrt(nc * VOX)),...]
    unnamed x4 -> x0, waiting for transfers between devices: 50.6 us -> none
    unnamed x272 -> x12, local copies, waits for them, and re-layouts: 55.8 us -> 5.8 us
    reduce_scatter x1 -> x0, waiting for transfers between devices: 41.7 us -> none  [on_device(): lax.psum_scatter(conv_rows(all_filters, own_padded, planes), 'row', scatt...]
    reshape x28 -> x0, local copies, waits for them, and re-layouts: 28.9 us -> none  [the longest x27 28.3 us: tap_view(): return piece.reshape(padded.shape[0], planes * S * S)]
    slice x6 -> x0, local copies, waits for them, and re-layouts: 23 us -> none  [the longest x4 15.2 us: tap_view(): padded[:, depth:depth + planes, height:height + S, across:across + S]]
  transfers between devices with their start and end apart: 7 -> 0, of which waited for: 3 -> 0; matrix products, arithmetic and copies ran while one was open for 24% -> 0% of each run, Pallas kernels for 0% -> 0%
where the time goes in v1:
time: 70.8 us; the launch traced here: 70.5 us
  Pallas kernels  64.1 us (91%)
  local copies, waits for them, and re-layouts  5.8 us (8%)
    pallas_call x1, Pallas kernels, on_device(): pl.pallas_call(functools.partial(kernel, nc, 1.0 / math.sqrt(nc * VOX)),...  64.1 us
    unnamed x12, local copies, waits for them, and re-layouts  5.8 us

profile of v1, /device:TPU:1, one launch (start us, length us, event | category | flops | bytes accessed | tf_op | source)
XLA Modules:
  0.0 70.5 jit_solution(7048314649049178343)
XLA Ops:
  0.6 0.0 copy-start.3
  0.6 0.6 copy-done.3
  1.3 0.0 copy-start
  1.3 0.9 %copy-done = bf16[27,32,64]{2,1,0:T(8,128)(2,1)S(1)} copy-done((bf16[27,32,64]{2,1,0:T(8,128)(2,1)S(1)}, bf16[27,32,64]{2,1,0:T(8,128)(2,1)}, u32[]{:S(2)}) %copy-start) | copy-done | bytes 110616
  2.2 0.0 copy-start.1
  2.2 0.8 %copy-done.1 = bf16[32,1024]{1,0:T(8,128)(2,1)S(1)} copy-done((bf16[32,1024]{1,0:T(8,128)(2,1)S(1)}, bf16[32,1024]{1,0:T(8,128)(2,1)}, u32[]{:S(2)}) %copy-start.1) | copy-done | bytes 65560
  3.1 0.0 copy-start.2
  3.1 0.8 %copy-done.2 = bf16[32,1024]{1,0:T(8,128)(2,1)S(1)} copy-done((bf16[32,1024]{1,0:T(8,128)(2,1)S(1)}, bf16[32,1024]{1,0:T(8,128)(2,1)}, u32[]{:S(2)}) %copy-start.2) | copy-done | bytes 65560
  3.9 64.1 %shard_map.75 = (bf16[32,1024]{1,0:T(8,128)(2,1)S(1)}, bf16[32,1024]{1,0:T(8,128)(2,1)S(1)}, f32[27,32,64]{2,1,0:T(8,128)S(1)}, f32[1,32]{1,0:T(1,128)S(1)}) custom-call(bf16[32,1024]{1,0:T(8,128)(2,1)S(1)} %copy-done.1, bf16[27,32,64]{2,1,0:T(8,128)(2,1)S(1)} %copy-done, bf16[1,64]{1,0:T(2,128)(2,1)S(1)} %bitcast.2, bf16[32,1024]{1,0:T(8,128)(2,1)S(1)} %copy-done.2), custom_call_target="tpu_custom_call" | custom-call | tf_op jit(solution)/shard_map/pallas_call | solution.py:258
  68.0 0.6 copy.12
  68.6 0.6 copy.13
  69.3 0.8 %copy.14 = f32[27,32,64]{2,1,0:T(8,128)} copy(f32[27,32,64]{2,1,0:T(8,128)S(1)} %get-tuple-element.18) | data formatting | bytes 442368
  70.0 0.5 copy.15
Async XLA Ops:
  0.6 0.7 copy-start.3
  1.3 0.9 %copy-start = (bf16[27,32,64]{2,1,0:T(8,128)(2,1)S(1)}, bf16[27,32,64]{2,1,0:T(8,128)(2,1)}, u32[]{:S(2)}) copy-start(bf16[27,32,64]{2,1,0:T(8,128)(2,1)} %w_ref.1) | copy-start | bytes 331780
  2.2 0.8 %copy-start.1 = (bf16[32,1024]{1,0:T(8,128)(2,1)S(1)}, bf16[32,1024]{1,0:T(8,128)(2,1)}, u32[]{:S(2)}) copy-start(bf16[32,1024]{1,0:T(8,128)(2,1)} %vol_ref.1) | copy-start | bytes 196612
  3.1 0.8 %copy-start.2 = (bf16[32,1024]{1,0:T(8,128)(2,1)S(1)}, bf16[32,1024]{1,0:T(8,128)(2,1)}, u32[]{:S(2)}) copy-start(bf16[32,1024]{1,0:T(8,128)(2,1)} %cot_ref.1) | copy-start | bytes 196612

commit v2 on v1

v2 whole, which is shorter than its diff:
```python
import functools
import math

import jax
import jax.numpy as jnp
from jax import lax
from jax.experimental import pallas as pl
from jax.experimental.pallas import tpu as pltpu
from jax.sharding import PartitionSpec as P

S = 32
VOX = S * S
CH = 32
TAPS = 27
DEPTH = TAPS * CH
PADDED = 896
LAST = PADDED - 128
MESH = pl.DeviceIdType.MESH
BF16 = jnp.bfloat16
F32 = jnp.float32
VMEM_LIMIT = 56 * 1024 * 1024
NT = (((1,), (1,)), ((), ()))
TN = (((0,), (0,)), ((), ()))


def inside(coord, step):
    moved = coord + step
    return (moved >= 0) & (moved < S)


def moved_view(value, y, x, dy, dx):
    offset = dy * S + dx
    if offset:
        value = pltpu.roll(value, (-offset) % VOX, 1)
    if dy or dx:
        value = jnp.where(inside(y, dy) & inside(x, dx), value, 0.0)
    return value


def kernel(
    nc, norm_factor,
    vol_hbm, w_hbm, bias_hbm, cot_hbm,
    out_hbm, dgrad_hbm, wsum_hbm, bsum_hbm,
    w_own, bias_own, cot, wpad, wt_own, wg, xin, xcol, ypart, yrecv, g, wgp, wgz, wzsum, wgrecv, bsend, brecv,
    z, dsib, dsib_recv, dnear, dhalo, dhalo_recv, out_v, dgrad_v, wsum_v, bsum_v,
    load_sem, store_sem, x_send, x_recv, xs_send, xs_recv, w_send, w_recv, wf_send, wf_recv,
    y_send, y_recv, g_send, g_recv, b_send, b_recv, p_send, p_recv, pz_send, pz_recv, pf_send, pf_recv,
    d_send, d_recv, h_send, h_recv,
):
    row = lax.axis_index("row")
    col = lax.axis_index("col")
    q = row // 2
    k = row % 2
    sib = 2 * q + 1 - k
    ny = nc // 2
    ypos = col // 2
    zpos = col % 2
    pair = 2 * ypos + 1 - zpos
    up = (col + 1) % nc
    down = (col + nc - 1) % nc

    def rows(start, size=CH):
        return pl.ds(pl.multiple_of(start, CH), size)

    def y_col(step):
        return 2 * ((ypos + step + ny) % ny) + zpos

    def owner(dy, dz):
        zo = 1 - zpos if dz else zpos
        return 2 * ((ypos - dy + ny) % ny) + zo

    def remote(src, dst, send_sem, recv_sem, to_row, to_col):
        return pltpu.make_async_remote_copy(
            src_ref=src, dst_ref=dst, send_sem=send_sem, recv_sem=recv_sem,
            device_id=(to_row, to_col), device_id_type=MESH,
        )

    copies = []

    def send(*args):
        copy = remote(*args)
        copy.start()
        copies.append(copy)
        return copy

    load_w = pltpu.make_async_copy(w_hbm, w_own, load_sem.at[0])
    load_bias = pltpu.make_async_copy(bias_hbm, bias_own, load_sem.at[1])
    load_vol = pltpu.make_async_copy(vol_hbm, xin.at[1, rows(CH * k), :], load_sem.at[2])
    load_cot = pltpu.make_async_copy(cot_hbm, cot, load_sem.at[3])
    for load in (load_w, load_bias, load_vol, load_cot):
        load.start()

    barrier = pltpu.get_barrier_semaphore()
    peers = [(sib, col), (row, pair), (sib, pair)]
    peers += [(row, up), (row, down)]
    for dy in range(1, ny):
        peers += [(row, y_col(dy)), (sib, y_col(dy)), (row, 2 * ((ypos + dy) % ny) + 1 - zpos)]
    for j in range(1, nc):
        peers.append((2 * ((q + j) % nc) + k, col))
    for peer in peers:
        pl.semaphore_signal(barrier, inc=1, device_id=peer, device_id_type=MESH)

    wpad[...] = jnp.zeros_like(wpad)
    bsend[...] = jnp.zeros_like(bsend)
    load_w.wait()
    load_bias.wait()
    wpad[0:DEPTH, 0 : 2 * CH] = w_own[...].reshape(DEPTH, 2 * CH).astype(F32)
    wpad[DEPTH : DEPTH + 1, 0 : 2 * CH] = bias_own[...].astype(F32)
    wt_own[...] = jnp.transpose(wpad[...])[0 : 2 * CH].astype(BF16)
    load_vol.wait()
    mine, other = rows(CH * k), rows(CH * (1 - k))

    pl.semaphore_wait(barrier, len(peers))

    def slot(dy, dz):
        return CH * (dz * ny + dy)

    def slot_rows(dy, dz):
        return pl.ds(slot(dy, dz), CH)

    w_copies = {}

    def send_weights(dy, dz, to_col):
        for o in range(2):
            if (dy, dz, o) == (0, 0, 0):
                continue
            w_copies[dy, dz, o] = send(
                wt_own.at[other if o else mine, :], wg.at[k, slot_rows(dy, dz), :],
                w_send.at[dz * ny + dy, o], w_recv.at[dz * ny + dy, o], sib if o else row, to_col,
            )

    send_weights(0, 1, pair)
    x_sib = send(xin.at[1, mine, :], xin.at[1, mine, :], xs_send.at[1], xs_recv.at[1], sib, col)
    send_weights(0, 0, col)
    for dy in (1, 3, 2):
        if dy < ny:
            send_weights(dy, 0, y_col(dy))
    x_halo = {
        0: send(xin.at[1, mine, :], xin.at[0, mine, :], x_send.at[0], x_recv.at[0], row, up),
        2: send(xin.at[1, mine, :], xin.at[2, mine, :], x_send.at[2], x_recv.at[2], row, down),
    }
    wg[k, slot_rows(0, 0), :] = wt_own[mine, :]

    lane = lax.broadcasted_iota(jnp.int32, (CH, VOX), 1)
    y, x = lane // S, lane % S
    low_ok = (col > 0).astype(F32)
    high_ok = (col < nc - 1).astype(F32)
    for h in range(2):
        xcol[h, DEPTH:PADDED, :] = jnp.zeros((PADDED - DEPTH, VOX), BF16)

    def fill(a, h):
        plane = xin[a, rows(CH * h), :].astype(F32)
        if a == 0:
            plane = plane * low_ok
        if a == 2:
            plane = plane * high_ok
        for b in range(3):
            for c in range(3):
                tap = 9 * a + 3 * b + c
                xcol[h, CH * tap : CH * tap + CH, :] = moved_view(plane, y, x, b - 1, c - 1).astype(BF16)

    fill(1, k)
    for o in range(2):
        w_copies[0, 1, o].wait_recv()
    wf_copies = []
    for dy in (1, 3, 2):
        if dy < ny:
            wf_copies.append(
                send(
                    wg.at[:, slot_rows(0, 1), :], wg.at[:, slot_rows(dy, 1), :],
                    wf_send.at[dy], wf_recv.at[dy], row, y_col(dy),
                )
            )
    x_sib.wait_recv()
    fill(1, 1 - k)
    x_forward = {}
    for a in (0, 2):
        x_halo[a].wait_recv()
        x_forward[a] = send(xin.at[a, mine, :], xin.at[a, mine, :], xs_send.at[a], xs_recv.at[a], sib, col)
    for a in (0, 2):
        fill(a, k)
    for a in (0, 2):
        x_forward[a].wait_recv()
        fill(a, 1 - k)

    later = []
    for dz in range(2):
        if dz == 0:
            w_copies[0, 0, 1].wait_recv()
            for dy in range(1, ny):
                for o in range(2):
                    w_copies[dy, 0, o].wait_recv()
        else:
            for copy in wf_copies:
                copy.wait_recv()
        half = pl.ds(CH * ny * dz, CH * ny)
        ypart[half, :] = (
            jnp.dot(wg[0, half, :], xcol[0], preferred_element_type=F32)
            + jnp.dot(wg[1, half, :], xcol[1], preferred_element_type=F32)
        ).astype(BF16)
        for dy in range(ny):
            to = owner(dy, dz)
            copy = remote(
                ypart.at[slot_rows(dy, dz), :], yrecv.at[q],
                y_send.at[dz * ny + dy], y_recv.at[q], 2 * to + k, col,
            )

            @pl.when(to != q)
            def _():
                copy.start()

            later.append((to != q, copy))

    def from_pair(index, dst, sem):
        return remote(dst, dst, sem, sem, 2 * index + k, col)

    own_slot = rows(CH * ((q % 2 != zpos).astype(jnp.int32) * ny + (ypos - q // 2 + ny) % ny))
    sectioned = ypart[own_slot, :].astype(F32)
    tail = wg[0, own_slot, LAST:PADDED].astype(F32)
    tail_lane = lax.broadcasted_iota(jnp.int32, (CH, 128), 1)
    own_bias = jnp.sum(jnp.where(tail_lane == DEPTH - LAST, tail, 0.0), axis=1, keepdims=True)
    load_cot.wait()
    for j in range(1, nc):
        source = (q + j) % nc
        from_pair(source, yrecv.at[source], y_recv.at[source]).wait_recv()
    for j in range(1, nc):
        sectioned = sectioned + yrecv[(q + j) % nc].astype(F32)
    sectioned = sectioned + own_bias
    s = 1.0 / (1.0 + jnp.exp(-sectioned))
    g[own_slot, :] = (cot[...].astype(F32) * (s * (1.0 + sectioned * (1.0 - s)))).astype(BF16)
    for j in range(1, nc):
        send(g.at[own_slot, :], g.at[own_slot, :], g_send.at[j], g_recv.at[q], 2 * ((q + j) % nc) + k, col)
    out_v[...] = (sectioned * s).astype(BF16)
    store_out = pltpu.make_async_copy(out_v, out_hbm, store_sem.at[0])
    store_out.start()

    bsend[:, 0:CH] = lax.dot_general(jnp.ones((8, VOX), BF16), g[own_slot, :], NT, preferred_element_type=F32)
    b_copies = []
    for d in range(1, nc):
        b_copies.append(send(bsend, brecv.at[d], b_send.at[d], b_recv.at[d], row, (col + d) % nc))

    p_copies = []
    pf_copies = []
    for dz in (1, 0):
        for dy in range(ny):
            source = owner(dy, dz)

            @pl.when(source != q)
            def _():
                part = g.at[slot_rows(dy, dz), :]
                from_pair(source, part, g_recv.at[source]).wait_recv()

        half = pl.ds(CH * ny * dz, CH * ny)
        for h in range(2):
            wgp[h, half, :] = lax.dot_general(g[half, :], xcol[h], NT, preferred_element_type=F32).astype(BF16)
        for dy in (1, 3, 2, 0):
            if dy >= ny:
                continue
            if dz and dy:
                p_copies.append(
                    send(
                        wgp.at[:, slot_rows(dy, 1), :], wgz.at[dy],
                        p_send.at[dy], p_recv.at[dy], row, y_col(-dy),
                    )
                )
            elif not dz:
                for o in range(2):
                    if dy or o:
                        pf_copies.append(
                            send(
                                wgp.at[1 - k if o else k, slot_rows(dy, 0), :], wgrecv.at[dy, mine, :],
                                pf_send.at[dy, o], pf_recv.at[dy, o], sib if o else row, y_col(-dy),
                            )
                        )
    wgrecv[0, mine, :] = wgp[k, slot_rows(0, 0), :]

    def spread(h):
        z[...] = lax.dot_general(wg[h], g[...], TN, preferred_element_type=F32)
        planes = []
        for a in range(3):
            total = jnp.zeros((CH, VOX), F32)
            for b in range(3):
                for c in range(3):
                    tap = 9 * a + 3 * b + c
                    total = total + moved_view(z[CH * tap : CH * tap + CH, :], y, x, 1 - b, 1 - c)
            planes.append(total)
        return planes

    for a, total in enumerate(spread(1 - k)):
        dsib[a] = total.astype(BF16)
    d_copy = send(dsib, dsib_recv, d_send.at[0], d_recv.at[0], sib, col)

    for copy in p_copies:
        copy.wait_recv()
    for h in range(2):
        total = wgp[h, slot_rows(0, 1), :].astype(F32)
        for dy in range(1, ny):
            total = total + wgz[dy, h].astype(F32)
        wzsum[h] = total.astype(BF16)
    for o in range(2):
        pf_copies.append(
            send(
                wzsum.at[1 - k if o else k], wgrecv.at[ny, mine, :],
                pz_send.at[o], pz_recv.at[o], sib if o else row, pair,
            )
        )

    for a, total in enumerate(spread(k)):
        dnear[a] = total
    d_copy.wait_recv()
    h_copies = []
    for a, to_col in ((0, down), (2, up)):
        dhalo[a] = (dnear[a] + dsib_recv[a].astype(F32)).astype(BF16)
        h_copies.append(send(dhalo.at[a], dhalo_recv.at[a], h_send.at[a], h_recv.at[a], row, to_col))
    near = dnear[1] + dsib_recv[1].astype(F32)

    for copy in b_copies:
        copy.wait_recv()
    bias_sum = bsend[...]
    for d in range(1, nc):
        bias_sum = bias_sum + brecv[d]
    bsum_v[...] = bias_sum * norm_factor
    store_bias = pltpu.make_async_copy(bsum_v, bsum_hbm, store_sem.at[3])
    store_bias.start()

    for copy in h_copies:
        copy.wait_recv()
    near = near + low_ok * dhalo_recv[2].astype(F32) + high_ok * dhalo_recv[0].astype(F32)
    dgrad_v[...] = near.astype(BF16)
    store_data = pltpu.make_async_copy(dgrad_v, dgrad_hbm, store_sem.at[1])
    store_data.start()

    for copy in pf_copies:
        copy.wait_recv()
    total = wgrecv[0].astype(F32)
    for d in range(1, ny + 1):
        total = total + wgrecv[d].astype(F32)
    wsum_v[...] = total * norm_factor
    store_weights = pltpu.make_async_copy(wsum_v, wsum_hbm, store_sem.at[2])
    store_weights.start()

    for copy in copies:
        copy.wait_send()
    for sent, copy in later:

        @pl.when(sent)
        def _():
            copy.wait_send()

    for store in (store_out, store_data, store_weights, store_bias):
        store.wait()


def finish(
    out_in, dgrad_in, wsum_in, bsum_in, out_hbm, dgrad_hbm, wgrad_hbm, bgrad_hbm,
    out_v, dgrad_v, wsum_v, bsum_v, wgrad_v, bgrad_v, load_sem, store_sem,
):
    loads = [
        pltpu.make_async_copy(src, dst, load_sem.at[i])
        for i, (src, dst) in enumerate(
            ((wsum_in, wsum_v), (out_in, out_v), (dgrad_in, dgrad_v), (bsum_in, bsum_v))
        )
    ]
    stores = [
        pltpu.make_async_copy(src, dst, store_sem.at[i])
        for i, (src, dst) in enumerate(
            ((wgrad_v, wgrad_hbm), (out_v, out_hbm), (dgrad_v, dgrad_hbm), (bgrad_v, bgrad_hbm))
        )
    ]
    for load in loads:
        load.start()
    for i in (1, 2):
        loads[i].wait()
        stores[i].start()
    loads[3].wait()
    bgrad_v[...] = bsum_v[0:1, 0:CH]
    stores[3].start()
    loads[0].wait()
    wgrad_v[...] = jnp.transpose(wsum_v[...])[0:DEPTH].reshape(TAPS, CH, 2 * CH)
    stores[0].start()
    for store in stores:
        store.wait()


def on_device(nc, volume, filters, bias, cotangent):
    ny = nc // 2
    chunk = CH * nc
    dma = pltpu.SemaphoreType.DMA
    hbm = pl.BlockSpec(memory_space=pl.ANY)
    plane = (CH, VOX)
    sums = pl.pallas_call(
        functools.partial(kernel, nc, 1.0 / math.sqrt(nc * VOX)),
        out_shape=(
            jax.ShapeDtypeStruct(plane, BF16),
            jax.ShapeDtypeStruct(plane, BF16),
            jax.ShapeDtypeStruct((2 * CH, PADDED), F32),
            jax.ShapeDtypeStruct((8, 128), F32),
        ),
        in_specs=[hbm] * 4,
        out_specs=(hbm,) * 4,
        scratch_shapes=[
            pltpu.VMEM((TAPS, CH, 2 * CH), BF16),
            pltpu.VMEM((1, 2 * CH), BF16),
            pltpu.VMEM(plane, BF16),
            pltpu.VMEM((PADDED, 128), F32),
            pltpu.VMEM((2 * CH, PADDED), BF16),
            pltpu.VMEM((2, chunk, PADDED), BF16),
            pltpu.VMEM((3, 2 * CH, VOX), BF16),
            pltpu.VMEM((2, PADDED, VOX), BF16),
            pltpu.VMEM((chunk, VOX), BF16),
            pltpu.VMEM((nc, CH, VOX), BF16),
            pltpu.VMEM((chunk, VOX), BF16),
            pltpu.VMEM((2, chunk, PADDED), BF16),
            pltpu.VMEM((ny, 2, CH, PADDED), BF16),
            pltpu.VMEM((2, CH, PADDED), BF16),
            pltpu.VMEM((ny + 1, 2 * CH, PADDED), BF16),
            pltpu.VMEM((8, 128), F32),
            pltpu.VMEM((nc, 8, 128), F32),
            pltpu.VMEM((PADDED, VOX), F32),
            pltpu.VMEM((3, CH, VOX), BF16),
            pltpu.VMEM((3, CH, VOX), BF16),
            pltpu.VMEM((3, CH, VOX), F32),
            pltpu.VMEM((3, CH, VOX), BF16),
            pltpu.VMEM((3, CH, VOX), BF16),
            pltpu.VMEM(plane, BF16),
            pltpu.VMEM(plane, BF16),
            pltpu.VMEM((2 * CH, PADDED), F32),
            pltpu.VMEM((8, 128), F32),
            dma((4,)), dma((4,)),
            dma((3,)), dma((3,)), dma((3,)), dma((3,)),
            dma((nc, 2)), dma((nc, 2)), dma((ny,)), dma((ny,)),
            dma((nc,)), dma((nc,)), dma((nc,)), dma((nc,)), dma((nc,)), dma((nc,)),
            dma((ny,)), dma((ny,)), dma((2,)), dma((2,)), dma((ny, 2)), dma((ny, 2)),
            dma((1,)), dma((1,)), dma((3,)), dma((3,)),
        ],
        compiler_params=pltpu.CompilerParams(
            collective_id=0, has_side_effects=True, vmem_limit_bytes=VMEM_LIMIT
        ),
    )(volume, filters, bias.reshape(1, 2 * CH), cotangent)
    output, data_grad, weight_grad, bias_grad = pl.pallas_call(
        finish,
        out_shape=(
            jax.ShapeDtypeStruct(plane, BF16),
            jax.ShapeDtypeStruct(plane, BF16),
            jax.ShapeDtypeStruct((TAPS, CH, 2 * CH), F32),
            jax.ShapeDtypeStruct((1, CH), F32),
        ),
        in_specs=[hbm] * 4,
        out_specs=(hbm,) * 4,
        scratch_shapes=[
            pltpu.VMEM(plane, BF16),
            pltpu.VMEM(plane, BF16),
            pltpu.VMEM((2 * CH, PADDED), F32),
            pltpu.VMEM((8, 128), F32),
            pltpu.VMEM((TAPS, CH, 2 * CH), F32),
            pltpu.VMEM((1, CH), F32),
            dma((4,)), dma((4,)),
        ],
        compiler_params=pltpu.CompilerParams(vmem_limit_bytes=VMEM_LIMIT),
    )(*sums)
    return output, data_grad, weight_grad, bias_grad.reshape(CH)


def solution(mesh):
    placed = (P("row", "col"), P(None, "row", "col"), P("col"), P("row", "col"))
    return jax.shard_map(
        functools.partial(on_device, mesh.shape["col"]),
        mesh=mesh,
        in_specs=placed,
        out_specs=(P("row", "col"), P("row", "col"), P(None, "row", "col"), P("row")),
        check_vma=False,
    )
```

time: 70.8 us -> 59.8 us (0.84)
  local copies, waits for them, and re-layouts: 5.8 us -> 0 us
  Pallas kernels: 64.1 us -> 58.3 us
    pallas_call x1, Pallas kernels: 64.1 us -> 56.2 us  [on_device(): pl.pallas_call(functools.partial(kernel, nc, 1.0 / math.sqrt(nc * VOX)),...]
    unnamed x12 -> x0, local copies, waits for them, and re-layouts: 5.8 us -> none
    pallas_call x0 -> x1, Pallas kernels: none -> 2.02 us  [on_device(): pl.pallas_call(finish, out_shape=(jax.ShapeDtypeStruct(plane, BF16), jax....]
where the time goes in v2:
time: 59.8 us; the launch traced here: 58.9 us
  Pallas kernels  58.3 us (97%)
  between operations  0.64 us (1%)
    pallas_call x1, Pallas kernels, on_device(): pl.pallas_call(functools.partial(kernel, nc, 1.0 / math.sqrt(nc * VOX)),...  56.2 us
    pallas_call x1, Pallas kernels, on_device(): pl.pallas_call(finish, out_shape=(jax.ShapeDtypeStruct(plane, BF16), jax....  2.02 us

profile of v2, /device:TPU:1, one launch (start us, length us, event | category | flops | bytes accessed | tf_op | source)
XLA Modules:
  0.0 58.9 jit_solution(14888174001445865342)
XLA Ops:
  0.6 56.2 %shard_map.75 = (bf16[32,1024]{1,0:T(8,128)(2,1)}, bf16[32,1024]{1,0:T(8,128)(2,1)}, f32[64,896]{1,0:T(8,128)}, f32[8,128]{1,0:T(8,128)}) custom-call(bf16[32,1024]{1,0:T(8,128)(2,1)} %vol_hbm.1, bf16[27,32,64]{2,1,0:T(8,128)(2,1)} %w_hbm.1, bf16[1,64]{1,0:T(2,128)(2,1)} %bitcast.2, bf16[32,1024]{1,0:T(8,128)(2,1)} %cot_hbm.1), custom_call_target="tpu_custom_call" | custom-call | tf_op jit(solution)/shard_map/pallas_call | solution.py:391
  56.9 2.0 %shard_map.76 = (bf16[32,1024]{1,0:T(8,128)(2,1)}, bf16[32,1024]{1,0:T(8,128)(2,1)}, f32[27,32,64]{2,1,0:T(8,128)}, f32[1,32]{1,0:T(1,128)}) custom-call(bf16[32,1024]{1,0:T(8,128)(2,1)} %get-tuple-element.12.out_in, bf16[32,1024]{1,0:T(8,128)(2,1)} %get-tuple-element.13.dgrad_in, f32[64,896]{1,0:T(8,128)} %get-tuple-element.14.wsum_in, ...), custom_call_target="tpu_custom_call" | custom-call | tf_op jit(solution)/shard_map/pallas_call | solution.py:440

commit v3 on v2

v3 whole, which is shorter than its diff:
```python
import functools
import math

import jax
import jax.numpy as jnp
from jax import lax
from jax.experimental import pallas as pl
from jax.experimental.pallas import tpu as pltpu
from jax.sharding import PartitionSpec as P

S = 32
VOX = S * S
CH = 32
TAPS = 27
DEPTH = TAPS * CH
HALF = CH // 2
VIEWS = 9 * CH
PADDED = 896
LAST = PADDED - 128
MESH = pl.DeviceIdType.MESH
BF16 = jnp.bfloat16
F32 = jnp.float32
VMEM_LIMIT = 56 * 1024 * 1024
NT = (((1,), (1,)), ((), ()))
TN = (((0,), (0,)), ((), ()))


def inside(coord, step):
    moved = coord + step
    return (moved >= 0) & (moved < S)


def moved_view(value, y, x, dy, dx):
    offset = dy * S + dx
    if offset:
        value = pltpu.roll(value, (-offset) % VOX, 1)
    if dy or dx:
        value = jnp.where(inside(y, dy) & inside(x, dx), value, 0.0)
    return value


def kernel(
    nc, norm_factor,
    vol_hbm, w_hbm, bias_hbm, cot_hbm,
    out_hbm, dgrad_hbm, wsum_hbm, bsum_hbm,
    w_own, bias_own, cot, wpad, wt_own, wg, xin, xcol, ypart, yrecv, gown, g, wgp, wgrecv, bsend, brecv,
    z, dsib, dsib_recv, dnear, dfar, dfar_recv, out_v, dgrad_v, wsum_v, bsum_v,
    load_sem, store_sem, x_send, x_recv, xs_send, xs_recv, w_send, w_recv,
    y_send, y_recv, g_send, g_recv, b_send, b_recv, p_send, p_recv, d_send, d_recv, h_send, h_recv,
):
    row = lax.axis_index("row")
    col = lax.axis_index("col")
    q = row // 2
    k = row % 2
    sib = 2 * q + 1 - k
    ny = nc // 2
    xpos = q // 2
    zlow = q % 2
    ypos = col // 2
    zpos = col % 2
    pair = 2 * ypos + 1 - zpos

    def rows(start, size=CH):
        return pl.ds(pl.multiple_of(start, CH), size)

    def around(position):
        return (position + 2 * ny) % ny

    def half_rows(start):
        return pl.ds(pl.multiple_of(start, HALF), HALF)

    def flip(position, other_one):
        return 1 - position if other_one else position

    steps = [dx for dx in (1, 3, 2, 0) if dx < ny]
    col_steps = [(dy, dz) for dy in steps for dz in (1, 0)]
    row_steps = [(dx, a, p) for dx in steps for a in (1, 0) for p in (1, 0)]

    def col_at(dy, dz):
        return 2 * around(ypos + dy) + flip(zpos, dz)

    def pair_at(dx, a):
        return 2 * around(xpos + dx) + flip(zlow, a)

    def remote(src, dst, send_sem, recv_sem, to_row, to_col):
        return pltpu.make_async_remote_copy(
            src_ref=src, dst_ref=dst, send_sem=send_sem, recv_sem=recv_sem,
            device_id=(to_row, to_col), device_id_type=MESH,
        )

    copies = []

    def send(*args):
        copy = remote(*args)
        copy.start()
        copies.append(copy)
        return copy

    def arrived(dst, sem):
        remote(dst, dst, sem, sem, sib, col).wait_recv()

    load_w = pltpu.make_async_copy(w_hbm, w_own, load_sem.at[0])
    load_bias = pltpu.make_async_copy(bias_hbm, bias_own, load_sem.at[1])
    mine, other = rows(CH * k), rows(CH * (1 - k))
    load_vol = pltpu.make_async_copy(vol_hbm, xin.at[1 + zpos, mine, :], load_sem.at[2])
    load_cot = pltpu.make_async_copy(cot_hbm, cot, load_sem.at[3])
    for load in (load_w, load_bias, load_vol, load_cot):
        load.start()

    barrier = pltpu.get_barrier_semaphore()
    peers = [(sib if o else row, col_at(dy, dz)) for dy, dz in col_steps for o in range(2) if dy or dz or o]
    peers += [(2 * pair_at(dx, a) + k, 2 * ypos + flip(zpos, p)) for dx, a, p in row_steps if dx or a or p]
    for peer in peers:
        pl.semaphore_signal(barrier, inc=1, device_id=peer, device_id_type=MESH)

    wpad[...] = jnp.zeros_like(wpad)
    bsend[...] = jnp.zeros_like(bsend)
    wgp[:, :, LAST:PADDED] = jnp.zeros((2, HALF * nc, 128), BF16)
    load_w.wait()
    load_bias.wait()
    wpad[0:DEPTH, 0 : 2 * CH] = w_own[...].reshape(DEPTH, 2 * CH).astype(F32)
    wpad[DEPTH : DEPTH + 1, 0 : 2 * CH] = bias_own[...].astype(F32)
    wt_own[...] = jnp.transpose(wpad[...])[0 : 2 * CH].astype(BF16)
    load_vol.wait()

    pl.semaphore_wait(barrier, len(peers))

    own_plane = xin.at[1 + zpos, mine, :]
    x_sib = send(own_plane, own_plane, xs_send.at[0], xs_recv.at[0], sib, col)
    x_pair = send(own_plane, own_plane, x_send.at[0], x_recv.at[0], row, pair)
    side = around(ypos + 2 * zpos - 1)
    edge = xin.at[3 - 3 * zpos, mine, :]
    for i in range(2):
        send(own_plane, edge, x_send.at[1 + i], x_recv.at[2 - zpos], row, 2 * side + (zpos + i) % 2)

    own_rows = half_rows(HALF * col)
    w_copies = []
    for dy, dz in col_steps:
        for o in range(2):
            if dy or dz or o:
                part = half_rows(CH * flip(k, o) + HALF * flip(zpos, dz))
                w_copies.append(
                    send(
                        wt_own.at[part, :], wg.at[k, own_rows, :],
                        w_send.at[dy, dz, o], w_recv.at[dy, dz, o], sib if o else row, col_at(dy, dz),
                    )
                )
    wg[k, own_rows, :] = wt_own[half_rows(CH * k + HALF * zpos), :]

    lane = lax.broadcasted_iota(jnp.int32, (CH, VOX), 1)
    y, x = lane // S, lane % S
    low_ok = (ypos > 0).astype(F32)
    high_ok = (ypos < ny - 1).astype(F32)

    def fill(m, h, ok=None):
        plane = xin[m, rows(CH * h), :].astype(F32)
        if ok is not None:
            plane = plane * ok
        for b in range(3):
            for c in range(3):
                start = VIEWS * m + CH * (3 * b + c)
                xcol[h, rows(start), :] = moved_view(plane, y, x, b - 1, c - 1).astype(BF16)

    fill(1 + zpos, k)
    x_sib.wait_recv()
    fill(1 + zpos, 1 - k)
    to_sib = []
    x_pair.wait_recv()
    part = xin.at[2 - zpos, mine, :]
    to_sib.append(send(part, part, xs_send.at[1], xs_recv.at[1], sib, col))
    for i, m in ((1, 0), (2, 3)):
        part = xin.at[m, mine, :]
        arrived(part, x_recv.at[i])
        to_sib.append(send(part, part, xs_send.at[1 + i], xs_recv.at[1 + i], sib, col))
    fill(2 - zpos, k)
    fill(0, k, low_ok)
    fill(3, k, high_ok)
    for copy, m, ok in zip(to_sib, (2 - zpos, 0, 3), (None, low_ok, high_ok)):
        copy.wait_recv()
        fill(m, 1 - k, ok)

    chunk = HALF * nc
    for copy in w_copies:
        copy.wait_recv()
    tail = wg[0, :, LAST:PADDED].astype(F32)
    tail_lane = lax.broadcasted_iota(jnp.int32, (chunk, 128), 1)
    tail_row = lax.broadcasted_iota(jnp.int32, (chunk, 128), 0)
    with_bias = (tail_lane == DEPTH - LAST) & (tail_row // HALF == q)
    chunk_bias = jnp.sum(jnp.where(with_bias, tail, 0.0), axis=1, keepdims=True)
    for p in range(2):
        taps = pl.ds(VIEWS * p, DEPTH)
        ypart[p] = (
            jnp.dot(wg[0, :, 0:DEPTH], xcol[0, taps, :], preferred_element_type=F32)
            + jnp.dot(wg[1, :, 0:DEPTH], xcol[1, taps, :], preferred_element_type=F32)
            + chunk_bias
        ).astype(BF16)
    y_copies = []
    for dx, a, p in row_steps:
        to = pair_at(dx, a)
        plane = flip(zpos, p)
        part = half_rows(HALF * to)
        if dx or a or p:
            y_copies.append(
                send(
                    ypart.at[plane, part, :], yrecv.at[2 * dx + a, half_rows(HALF * zpos), :],
                    y_send.at[2 * dx + a, p], y_recv.at[2 * dx + a, p], 2 * to + k, 2 * ypos + plane,
                )
            )
        else:
            yrecv[0, half_rows(HALF * zpos), :] = ypart[plane, part, :]

    load_cot.wait()
    for copy in y_copies:
        copy.wait_recv()
    sectioned = yrecv[0].astype(F32)
    for j in range(1, nc):
        sectioned = sectioned + yrecv[j].astype(F32)
    s = 1.0 / (1.0 + jnp.exp(-sectioned))
    gown[...] = (cot[...].astype(F32) * (s * (1.0 + sectioned * (1.0 - s)))).astype(BF16)
    g_copies = []
    own_rows = half_rows(HALF * q)
    for dx, a, p in row_steps:
        part = half_rows(HALF * flip(zpos, p))
        if dx or a or p:
            g_copies.append(
                send(
                    gown.at[part, :], g.at[zpos, own_rows, :], g_send.at[2 * dx + a, p], g_recv.at[2 * dx + a, p],
                    2 * pair_at(dx, a) + k, 2 * ypos + flip(zpos, p),
                )
            )
        else:
            g[zpos, own_rows, :] = gown[part, :]

    out_v[...] = (sectioned * s).astype(BF16)
    store_out = pltpu.make_async_copy(out_v, out_hbm, store_sem.at[0])
    store_out.start()
    bsend[:, 0:CH] = lax.dot_general(jnp.ones((8, VOX), BF16), gown[...], NT, preferred_element_type=F32)
    b_copies = []
    for d in range(1, nc):
        b_copies.append(send(bsend, brecv.at[d], b_send.at[d], b_recv.at[d], row, (col + d) % nc))

    for copy in g_copies:
        copy.wait_recv()
    for h in range(2):
        total = jnp.zeros((chunk, DEPTH), F32)
        for p in range(2):
            total = total + lax.dot_general(
                g[p], xcol[h, VIEWS * p : VIEWS * p + DEPTH, :], NT, preferred_element_type=F32
            )
        wgp[h, :, 0:DEPTH] = total.astype(BF16)
    p_copies = []
    place = half_rows(CH * k + HALF * zpos)
    for dy, dz in col_steps:
        to = col_at(dy, dz)
        part = half_rows(HALF * to)
        for o in range(2):
            if dy or dz or o:
                p_copies.append(
                    send(
                        wgp.at[flip(k, o), part, :], wgrecv.at[dy, place, :],
                        p_send.at[dy, dz, o], p_recv.at[dy, dz, o], sib if o else row, to,
                    )
                )
            else:
                wgrecv[0, place, :] = wgp[k, part, :]

    def spread(h):
        for p in range(2):
            z[p] = lax.dot_general(wg[h], g[p], TN, preferred_element_type=F32)
        planes = []
        for m in range(4):
            total = jnp.zeros((CH, VOX), F32)
            for b in range(3):
                for c in range(3):
                    part = None
                    for p in range(2):
                        if 0 <= m - p <= 2:
                            start = VIEWS * (m - p) + CH * (3 * b + c)
                            term = z[p, start : start + CH, :]
                            part = term if part is None else part + term
                    total = total + moved_view(part, y, x, 1 - b, 1 - c)
            planes.append(total)
        return planes

    for m, total in enumerate(spread(1 - k)):
        dsib[m] = total.astype(BF16)
    d_copy = send(dsib, dsib_recv, d_send.at[0], d_recv.at[0], sib, col)
    for m, total in enumerate(spread(k)):
        dnear[m] = total
    d_copy.wait_recv()
    for m in range(4):
        dnear[m] = dnear[m] + dsib_recv[m].astype(F32)
    dfar[0] = dnear[0].astype(BF16)
    dfar[1] = dnear[2 - zpos].astype(BF16)
    dfar[2] = dnear[3].astype(BF16)
    send(dfar.at[0], dfar_recv.at[1 + zpos], h_send.at[0], h_recv.at[1 + zpos], row, 2 * around(ypos - 1) + 1)
    send(dfar.at[1], dfar_recv.at[0], h_send.at[1], h_recv.at[0], row, pair)
    send(dfar.at[2], dfar_recv.at[1 + zpos], h_send.at[2], h_recv.at[1 + zpos], row, 2 * around(ypos + 1))

    for copy in b_copies:
        copy.wait_recv()
    bias_sum = bsend[...]
    for d in range(1, nc):
        bias_sum = bias_sum + brecv[d]
    bsum_v[...] = bias_sum * norm_factor
    store_bias = pltpu.make_async_copy(bsum_v, bsum_hbm, store_sem.at[3])
    store_bias.start()

    for i in range(3):
        arrived(dfar_recv.at[i], h_recv.at[i])
    edge_ok = jnp.where(zpos == 1, high_ok, low_ok)
    near_sum = dnear[1 + zpos] + dfar_recv[0].astype(F32)
    near_sum = near_sum + edge_ok * (dfar_recv[1].astype(F32) + dfar_recv[2].astype(F32))
    dgrad_v[...] = near_sum.astype(BF16)
    store_data = pltpu.make_async_copy(dgrad_v, dgrad_hbm, store_sem.at[1])
    store_data.start()

    for copy in p_copies:
        copy.wait_recv()
    total = wgrecv[0].astype(F32)
    for d in range(1, ny):
        total = total + wgrecv[d].astype(F32)
    wsum_v[...] = total * norm_factor
    store_weights = pltpu.make_async_copy(wsum_v, wsum_hbm, store_sem.at[2])
    store_weights.start()

    for copy in copies:
        copy.wait_send()
    for store in (store_out, store_data, store_weights, store_bias):
        store.wait()


def finish(
    out_in, dgrad_in, wsum_in, bsum_in, out_hbm, dgrad_hbm, wgrad_hbm, bgrad_hbm,
    out_v, dgrad_v, wsum_v, bsum_v, wgrad_v, bgrad_v, load_sem, store_sem,
):
    loads = [
        pltpu.make_async_copy(src, dst, load_sem.at[i])
        for i, (src, dst) in enumerate(
            ((wsum_in, wsum_v), (out_in, out_v), (dgrad_in, dgrad_v), (bsum_in, bsum_v))
        )
    ]
    stores = [
        pltpu.make_async_copy(src, dst, store_sem.at[i])
        for i, (src, dst) in enumerate(
            ((wgrad_v, wgrad_hbm), (out_v, out_hbm), (dgrad_v, dgrad_hbm), (bgrad_v, bgrad_hbm))
        )
    ]
    for load in loads:
        load.start()
    for i in (1, 2):
        loads[i].wait()
        stores[i].start()
    loads[3].wait()
    bgrad_v[...] = bsum_v[0:1, 0:CH]
    stores[3].start()
    loads[0].wait()
    wgrad_v[...] = jnp.transpose(wsum_v[...])[0:DEPTH].reshape(TAPS, CH, 2 * CH)
    stores[0].start()
    for store in stores:
        store.wait()


def on_device(nc, volume, filters, bias, cotangent):
    ny = nc // 2
    chunk = HALF * nc
    dma = pltpu.SemaphoreType.DMA
    hbm = pl.BlockSpec(memory_space=pl.ANY)
    plane = (CH, VOX)
    sums = pl.pallas_call(
        functools.partial(kernel, nc, 1.0 / math.sqrt(nc * VOX)),
        out_shape=(
            jax.ShapeDtypeStruct(plane, BF16),
            jax.ShapeDtypeStruct(plane, BF16),
            jax.ShapeDtypeStruct((2 * CH, PADDED), F32),
            jax.ShapeDtypeStruct((8, 128), F32),
        ),
        in_specs=[hbm] * 4,
        out_specs=(hbm,) * 4,
        scratch_shapes=[
            pltpu.VMEM((TAPS, CH, 2 * CH), BF16),
            pltpu.VMEM((1, 2 * CH), BF16),
            pltpu.VMEM(plane, BF16),
            pltpu.VMEM((PADDED, 128), F32),
            pltpu.VMEM((2 * CH, PADDED), BF16),
            pltpu.VMEM((2, chunk, PADDED), BF16),
            pltpu.VMEM((4, 2 * CH, VOX), BF16),
            pltpu.VMEM((2, 4 * VIEWS, VOX), BF16),
            pltpu.VMEM((2, chunk, VOX), BF16),
            pltpu.VMEM((nc, CH, VOX), BF16),
            pltpu.VMEM(plane, BF16),
            pltpu.VMEM((2, chunk, VOX), BF16),
            pltpu.VMEM((2, chunk, PADDED), BF16),
            pltpu.VMEM((ny, 2 * CH, PADDED), BF16),
            pltpu.VMEM((8, 128), F32),
            pltpu.VMEM((nc, 8, 128), F32),
            pltpu.VMEM((2, PADDED, VOX), F32),
            pltpu.VMEM((4, CH, VOX), BF16),
            pltpu.VMEM((4, CH, VOX), BF16),
            pltpu.VMEM((4, CH, VOX), F32),
            pltpu.VMEM((3, CH, VOX), BF16),
            pltpu.VMEM((3, CH, VOX), BF16),
            pltpu.VMEM(plane, BF16),
            pltpu.VMEM(plane, BF16),
            pltpu.VMEM((2 * CH, PADDED), F32),
            pltpu.VMEM((8, 128), F32),
            dma((4,)), dma((4,)),
            dma((3,)), dma((3,)), dma((4,)), dma((4,)),
            dma((ny, 2, 2)), dma((ny, 2, 2)),
            dma((nc, 2)), dma((nc, 2)), dma((nc, 2)), dma((nc, 2)), dma((nc,)), dma((nc,)),
            dma((ny, 2, 2)), dma((ny, 2, 2)), dma((1,)), dma((1,)), dma((3,)), dma((3,)),
        ],
        compiler_params=pltpu.CompilerParams(
            collective_id=0, has_side_effects=True, vmem_limit_bytes=VMEM_LIMIT
        ),
    )(volume, filters, bias.reshape(1, 2 * CH), cotangent)
    output, data_grad, weight_grad, bias_grad = pl.pallas_call(
        finish,
        out_shape=(
            jax.ShapeDtypeStruct(plane, BF16),
            jax.ShapeDtypeStruct(plane, BF16),
            jax.ShapeDtypeStruct((TAPS, CH, 2 * CH), F32),
            jax.ShapeDtypeStruct((1, CH), F32),
        ),
        in_specs=[hbm] * 4,
        out_specs=(hbm,) * 4,
        scratch_shapes=[
            pltpu.VMEM(plane, BF16),
            pltpu.VMEM(plane, BF16),
            pltpu.VMEM((2 * CH, PADDED), F32),
            pltpu.VMEM((8, 128), F32),
            pltpu.VMEM((TAPS, CH, 2 * CH), F32),
            pltpu.VMEM((1, CH), F32),
            dma((4,)), dma((4,)),
        ],
        compiler_params=pltpu.CompilerParams(vmem_limit_bytes=VMEM_LIMIT),
    )(*sums)
    return output, data_grad, weight_grad, bias_grad.reshape(CH)


def solution(mesh):
    placed = (P("row", "col"), P(None, "row", "col"), P("col"), P("row", "col"))
    return jax.shard_map(
        functools.partial(on_device, mesh.shape["col"]),
        mesh=mesh,
        in_specs=placed,
        out_specs=(P("row", "col"), P("row", "col"), P(None, "row", "col"), P("row")),
        check_vma=False,
    )
```

time: 59.8 us -> 56 us (0.936); the launches traced: 58.9 us -> 55.8 us
  Pallas kernels: 58.3 us -> 55.2 us
    pallas_call x1, Pallas kernels: 56.2 us -> 53.1 us  [on_device(): pl.pallas_call(functools.partial(kernel, nc, 1.0 / math.sqrt(nc * VOX)),...]
where the time goes in v3:
time: 56 us; the launch traced here: 55.8 us
  Pallas kernels  55.2 us (99%)
  between operations  0.64 us (1%)
    pallas_call x1, Pallas kernels, on_device(): pl.pallas_call(functools.partial(kernel, nc, 1.0 / math.sqrt(nc * VOX)),...  53.1 us
    pallas_call x1, Pallas kernels, on_device(): pl.pallas_call(finish, out_shape=(jax.ShapeDtypeStruct(plane, BF16), jax....  2.02 us

profile of v3, /device:TPU:1, one launch (start us, length us, event | category | flops | bytes accessed | tf_op | source)
XLA Modules:
  0.0 55.8 jit_solution(4679592447321585544)
XLA Ops:
  0.6 53.1 %shard_map.75 = (bf16[32,1024]{1,0:T(8,128)(2,1)}, bf16[32,1024]{1,0:T(8,128)(2,1)}, f32[64,896]{1,0:T(8,128)}, f32[8,128]{1,0:T(8,128)}) custom-call(bf16[32,1024]{1,0:T(8,128)(2,1)} %vol_hbm.1, bf16[27,32,64]{2,1,0:T(8,128)(2,1)} %w_hbm.1, bf16[1,64]{1,0:T(2,128)(2,1)} %bitcast.2, bf16[32,1024]{1,0:T(8,128)(2,1)} %cot_hbm.1), custom_call_target="tpu_custom_call" | custom-call | tf_op jit(solution)/shard_map/pallas_call | solution.py:370
  53.8 2.0 %shard_map.76 = (bf16[32,1024]{1,0:T(8,128)(2,1)}, bf16[32,1024]{1,0:T(8,128)(2,1)}, f32[27,32,64]{2,1,0:T(8,128)}, f32[1,32]{1,0:T(1,128)}) custom-call(bf16[32,1024]{1,0:T(8,128)(2,1)} %get-tuple-element.12.out_in, bf16[32,1024]{1,0:T(8,128)(2,1)} %get-tuple-element.13.dgrad_in, f32[64,896]{1,0:T(8,128)} %get-tuple-element.14.wsum_in, ...), custom_call_target="tpu_custom_call" | custom-call | tf_op jit(solution)/shard_map/pallas_call | solution.py:417

commit v4 on v3

--- a/solution.py
+++ b/solution.py
@@ -82,6 +82,9 @@
     def pair_at(dx, a):
         return 2 * around(xpos + dx) + flip(zlow, a)
 
+    def place(along, half):
+        return half_rows(HALF * (ny * half + along))
+
     def remote(src, dst, send_sem, recv_sem, to_row, to_col):
         return pltpu.make_async_remote_copy(
             src_ref=src, dst_ref=dst, send_sem=send_sem, recv_sem=recv_sem,
@@ -116,36 +119,37 @@
     wpad[...] = jnp.zeros_like(wpad)
     bsend[...] = jnp.zeros_like(bsend)
     wgp[:, :, LAST:PADDED] = jnp.zeros((2, HALF * nc, 128), BF16)
+    load_vol.wait()
+
+    pl.semaphore_wait(barrier, len(peers))
+
+    own_plane = xin.at[1 + zpos, mine, :]
+    side = 2 * around(ypos + 2 * zpos - 1)
+    edge = xin.at[3 - 3 * zpos, mine, :]
+    for i in range(2):
+        send(own_plane, edge, x_send.at[1 + i], x_recv.at[2 - zpos], row, side + flip(zpos, 1 - i))
+    x_sib = send(own_plane, own_plane, xs_send.at[0], xs_recv.at[0], sib, col)
+    x_pair = send(own_plane, own_plane, x_send.at[0], x_recv.at[0], row, pair)
+
     load_w.wait()
     load_bias.wait()
     wpad[0:DEPTH, 0 : 2 * CH] = w_own[...].reshape(DEPTH, 2 * CH).astype(F32)
     wpad[DEPTH : DEPTH + 1, 0 : 2 * CH] = bias_own[...].astype(F32)
     wt_own[...] = jnp.transpose(wpad[...])[0 : 2 * CH].astype(BF16)
-    load_vol.wait()
-
-    pl.semaphore_wait(barrier, len(peers))
-
-    own_plane = xin.at[1 + zpos, mine, :]
-    x_sib = send(own_plane, own_plane, xs_send.at[0], xs_recv.at[0], sib, col)
-    x_pair = send(own_plane, own_plane, x_send.at[0], x_recv.at[0], row, pair)
-    side = around(ypos + 2 * zpos - 1)
-    edge = xin.at[3 - 3 * zpos, mine, :]
-    for i in range(2):
-        send(own_plane, edge, x_send.at[1 + i], x_recv.at[2 - zpos], row, 2 * side + (zpos + i) % 2)
-
-    own_rows = half_rows(HALF * col)
-    w_copies = []
-    for dy, dz in col_steps:
-        for o in range(2):
-            if dy or dz or o:
-                part = half_rows(CH * flip(k, o) + HALF * flip(zpos, dz))
-                w_copies.append(
-                    send(
-                        wt_own.at[part, :], wg.at[k, own_rows, :],
-                        w_send.at[dy, dz, o], w_recv.at[dy, dz, o], sib if o else row, col_at(dy, dz),
+
+    w_near, w_far = [], []
+    for dz in range(2):
+        for dy in (*steps[-1:], *steps[:-1]):
+            for o in (1, 0):
+                if dy or dz or o:
+                    part = half_rows(CH * flip(k, o) + HALF * flip(zpos, dz))
+                    (w_far if dz else w_near).append(
+                        send(
+                            wt_own.at[part, :], wg.at[k, place(ypos, dz), :],
+                            w_send.at[dy, dz, o], w_recv.at[dy, dz, o], sib if o else row, col_at(dy, dz),
+                        )
                     )
-                )
-    wg[k, own_rows, :] = wt_own[half_rows(CH * k + HALF * zpos), :]
+    wg[k, place(ypos, 0), :] = wt_own[half_rows(CH * k + HALF * zpos), :]
 
     lane = lax.broadcasted_iota(jnp.int32, (CH, VOX), 1)
     y, x = lane // S, lane % S
@@ -165,10 +169,7 @@
     x_sib.wait_recv()
     fill(1 + zpos, 1 - k)
     to_sib = []
-    x_pair.wait_recv()
-    part = xin.at[2 - zpos, mine, :]
-    to_sib.append(send(part, part, xs_send.at[1], xs_recv.at[1], sib, col))
-    for i, m in ((1, 0), (2, 3)):
+    for i, m in ((0, 2 - zpos), (1, 0), (2, 3)):
         part = xin.at[m, mine, :]
         arrived(part, x_recv.at[i])
         to_sib.append(send(part, part, xs_send.at[1 + i], xs_recv.at[1 + i], sib, col))
@@ -179,57 +180,72 @@
         copy.wait_recv()
         fill(m, 1 - k, ok)
 
-    chunk = HALF * nc
-    for copy in w_copies:
-        copy.wait_recv()
-    tail = wg[0, :, LAST:PADDED].astype(F32)
-    tail_lane = lax.broadcasted_iota(jnp.int32, (chunk, 128), 1)
-    tail_row = lax.broadcasted_iota(jnp.int32, (chunk, 128), 0)
-    with_bias = (tail_lane == DEPTH - LAST) & (tail_row // HALF == q)
-    chunk_bias = jnp.sum(jnp.where(with_bias, tail, 0.0), axis=1, keepdims=True)
-    for p in range(2):
-        taps = pl.ds(VIEWS * p, DEPTH)
-        ypart[p] = (
-            jnp.dot(wg[0, :, 0:DEPTH], xcol[0, taps, :], preferred_element_type=F32)
-            + jnp.dot(wg[1, :, 0:DEPTH], xcol[1, taps, :], preferred_element_type=F32)
-            + chunk_bias
-        ).astype(BF16)
-    y_copies = []
+    across = (zlow + zpos) % 2
+    half = HALF * ny
+    tail_lane = lax.broadcasted_iota(jnp.int32, (half, 128), 1)
+    tail_row = lax.broadcasted_iota(jnp.int32, (half, 128), 0)
+    later = []
+    for dz in range(2):
+        for copy in w_far if dz else w_near:
+            copy.wait_recv()
+        part = slice(half * dz, half * dz + half)
+        tail = wg[0, part, LAST:PADDED].astype(F32)
+        with_bias = (tail_lane == DEPTH - LAST) & (tail_row // HALF == xpos) & (across == dz)
+        chunk_bias = jnp.sum(jnp.where(with_bias, tail, 0.0), axis=1, keepdims=True)
+        other_low = (across + dz) % 2
+        for p in (1, 0):
+            plane = flip(zpos, p)
+            taps = rows(VIEWS * plane, DEPTH)
+            ypart[plane, part, :] = (
+                jnp.dot(wg[0, part, 0:DEPTH], xcol[0, taps, :], preferred_element_type=F32)
+                + jnp.dot(wg[1, part, 0:DEPTH], xcol[1, taps, :], preferred_element_type=F32)
+                + chunk_bias
+            ).astype(BF16)
+            for dx in steps:
+                to = 2 * around(xpos + dx) + flip(zpos, dz)
+                chunk = ypart.at[plane, place(around(xpos + dx), dz), :]
+                copy = remote(
+                    chunk, yrecv.at[2 * dx + other_low, half_rows(HALF * zpos), :],
+                    y_send.at[2 * dx + dz, p], y_recv.at[2 * dx + other_low, p], 2 * to + k, 2 * ypos + plane,
+                )
+                if dx or p:
+                    copy.start()
+                    copies.append(copy)
+                else:
+                    away = other_low == 1
+
+                    @pl.when(away)
+                    def _():
+                        copy.start()
+
+                    @pl.when(jnp.logical_not(away))
+                    def _():
+                        yrecv[0, half_rows(HALF * zpos), :] = ypart[plane, place(xpos, dz), :]
+
+                    later.append((away, copy))
+
+    load_cot.wait()
     for dx, a, p in row_steps:
-        to = pair_at(dx, a)
-        plane = flip(zpos, p)
-        part = half_rows(HALF * to)
         if dx or a or p:
-            y_copies.append(
-                send(
-                    ypart.at[plane, part, :], yrecv.at[2 * dx + a, half_rows(HALF * zpos), :],
-                    y_send.at[2 * dx + a, p], y_recv.at[2 * dx + a, p], 2 * to + k, 2 * ypos + plane,
-                )
-            )
-        else:
-            yrecv[0, half_rows(HALF * zpos), :] = ypart[plane, part, :]
-
-    load_cot.wait()
-    for copy in y_copies:
-        copy.wait_recv()
+            arrived(yrecv.at[2 * dx + a, half_rows(HALF * flip(zpos, p)), :], y_recv.at[2 * dx + a, p])
     sectioned = yrecv[0].astype(F32)
     for j in range(1, nc):
         sectioned = sectioned + yrecv[j].astype(F32)
     s = 1.0 / (1.0 + jnp.exp(-sectioned))
     gown[...] = (cot[...].astype(F32) * (s * (1.0 + sectioned * (1.0 - s)))).astype(BF16)
     g_copies = []
-    own_rows = half_rows(HALF * q)
     for dx, a, p in row_steps:
         part = half_rows(HALF * flip(zpos, p))
+        rows_there = place(xpos, (across + p) % 2)
         if dx or a or p:
             g_copies.append(
                 send(
-                    gown.at[part, :], g.at[zpos, own_rows, :], g_send.at[2 * dx + a, p], g_recv.at[2 * dx + a, p],
+                    gown.at[part, :], g.at[zpos, rows_there, :], g_send.at[2 * dx + a, p], g_recv.at[2 * dx + a, p],
                     2 * pair_at(dx, a) + k, 2 * ypos + flip(zpos, p),
                 )
             )
         else:
-            g[zpos, own_rows, :] = gown[part, :]
+            g[zpos, rows_there, :] = gown[part, :]
 
     out_v[...] = (sectioned * s).astype(BF16)
     store_out = pltpu.make_async_copy(out_v, out_hbm, store_sem.at[0])
@@ -241,28 +257,27 @@
 
     for copy in g_copies:
         copy.wait_recv()
-    for h in range(2):
-        total = jnp.zeros((chunk, DEPTH), F32)
+    p_copies = []
+    lands = half_rows(CH * k + HALF * zpos)
+    for o in (1, 0):
+        h = flip(k, o)
+        total = jnp.zeros((2 * half, DEPTH), F32)
         for p in range(2):
             total = total + lax.dot_general(
                 g[p], xcol[h, VIEWS * p : VIEWS * p + DEPTH, :], NT, preferred_element_type=F32
             )
         wgp[h, :, 0:DEPTH] = total.astype(BF16)
-    p_copies = []
-    place = half_rows(CH * k + HALF * zpos)
-    for dy, dz in col_steps:
-        to = col_at(dy, dz)
-        part = half_rows(HALF * to)
-        for o in range(2):
+        for dy, dz in col_steps:
+            part = place(around(ypos + dy), dz)
             if dy or dz or o:
                 p_copies.append(
                     send(
-                        wgp.at[flip(k, o), part, :], wgrecv.at[dy, place, :],
-                        p_send.at[dy, dz, o], p_recv.at[dy, dz, o], sib if o else row, to,
+                        wgp.at[h, part, :], wgrecv.at[dy, lands, :],
+                        p_send.at[dy, dz, o], p_recv.at[dy, dz, o], sib if o else row, col_at(dy, dz),
                     )
                 )
             else:
-                wgrecv[0, place, :] = wgp[k, part, :]
+                wgrecv[0, lands, :] = wgp[h, part, :]
 
     def spread(h):
         for p in range(2):
@@ -308,9 +323,9 @@
 
     for i in range(3):
         arrived(dfar_recv.at[i], h_recv.at[i])
-    edge_ok = jnp.where(zpos == 1, high_ok, low_ok)
+    cross_ok = jnp.where(zpos == 1, high_ok, low_ok)
     near_sum = dnear[1 + zpos] + dfar_recv[0].astype(F32)
-    near_sum = near_sum + edge_ok * (dfar_recv[1].astype(F32) + dfar_recv[2].astype(F32))
+    near_sum = near_sum + cross_ok * (dfar_recv[1].astype(F32) + dfar_recv[2].astype(F32))
     dgrad_v[...] = near_sum.astype(BF16)
     store_data = pltpu.make_async_copy(dgrad_v, dgrad_hbm, store_sem.at[1])
     store_data.start()
@@ -326,6 +341,12 @@
 
     for copy in copies:
         copy.wait_send()
+    for sent, copy in later:
+
+        @pl.when(sent)
+        def _():
+            copy.wait_send()
+
     for store in (store_out, store_data, store_weights, store_bias):
         store.wait()
 
@@ -334,29 +355,30 @@
     out_in, dgrad_in, wsum_in, bsum_in, out_hbm, dgrad_hbm, wgrad_hbm, bgrad_hbm,
     out_v, dgrad_v, wsum_v, bsum_v, wgrad_v, bgrad_v, load_sem, store_sem,
 ):
-    loads = [
-        pltpu.make_async_copy(src, dst, load_sem.at[i])
-        for i, (src, dst) in enumerate(
-            ((wsum_in, wsum_v), (out_in, out_v), (dgrad_in, dgrad_v), (bsum_in, bsum_v))
-        )
-    ]
-    stores = [
-        pltpu.make_async_copy(src, dst, store_sem.at[i])
-        for i, (src, dst) in enumerate(
-            ((wgrad_v, wgrad_hbm), (out_v, out_hbm), (dgrad_v, dgrad_hbm), (bgrad_v, bgrad_hbm))
-        )
-    ]
+    cut = (TAPS + 1) // 2 // 4 * 4 + 4
+    lanes = (slice(0, CH * cut), slice(CH * cut, PADDED))
+    taps = (slice(0, cut), slice(cut, TAPS))
+    loads = [pltpu.make_async_copy(wsum_in.at[:, lanes[i]], wsum_v.at[:, lanes[i]], load_sem.at[i]) for i in range(2)]
+    stores = [pltpu.make_async_copy(wgrad_v.at[taps[i]], wgrad_hbm.at[taps[i]], store_sem.at[i]) for i in range(2)]
+    small = ((out_in, out_v, out_hbm), (dgrad_in, dgrad_v, dgrad_hbm), (bsum_in, bsum_v, None))
+    for i, (src, dst, _) in enumerate(small):
+        loads.append(pltpu.make_async_copy(src, dst, load_sem.at[2 + i]))
     for load in loads:
         load.start()
-    for i in (1, 2):
+    for i in range(2):
         loads[i].wait()
+        part = jnp.transpose(wsum_v[:, lanes[i]])
+        count = taps[i].stop - taps[i].start
+        wgrad_v[taps[i]] = part[0 : CH * count].reshape(count, CH, 2 * CH)
         stores[i].start()
-    loads[3].wait()
+    for i, (_, src, dst) in enumerate(small[:2]):
+        loads[2 + i].wait()
+        stores.append(pltpu.make_async_copy(src, dst, store_sem.at[2 + i]))
+        stores[-1].start()
+    loads[4].wait()
     bgrad_v[...] = bsum_v[0:1, 0:CH]
-    stores[3].start()
-    loads[0].wait()
-    wgrad_v[...] = jnp.transpose(wsum_v[...])[0:DEPTH].reshape(TAPS, CH, 2 * CH)
-    stores[0].start()
+    stores.append(pltpu.make_async_copy(bgrad_v, bgrad_hbm, store_sem.at[4]))
+    stores[-1].start()
     for store in stores:
         store.wait()
 
@@ -431,7 +453,7 @@
             pltpu.VMEM((8, 128), F32),
             pltpu.VMEM((TAPS, CH, 2 * CH), F32),
             pltpu.VMEM((1, CH), F32),
-            dma((4,)), dma((4,)),
+            dma((5,)), dma((5,)),
         ],
         compiler_params=pltpu.CompilerParams(vmem_limit_bytes=VMEM_LIMIT),
     )(*sums)

time: 56 us -> 53.6 us (0.957)
  Pallas kernels: 55.2 us -> 52.8 us
    pallas_call x1, Pallas kernels: 53.1 us -> 50.8 us  [on_device(): pl.pallas_call(functools.partial(kernel, nc, 1.0 / math.sqrt(nc * VOX)),...]
where the time goes in v4:
time: 53.6 us; the launch traced here: 53.4 us
  Pallas kernels  52.8 us (99%)
  between operations  0.64 us (1%)
    pallas_call x1, Pallas kernels, on_device(): pl.pallas_call(functools.partial(kernel, nc, 1.0 / math.sqrt(nc * VOX)),...  50.8 us
    pallas_call x1, Pallas kernels, on_device(): pl.pallas_call(finish, out_shape=(jax.ShapeDtypeStruct(plane, BF16), jax....  1.97 us

profile of v4, /device:TPU:1, one launch (start us, length us, event | category | flops | bytes accessed | tf_op | source)
XLA Modules:
  0.0 53.4 jit_solution(9422861946989256234)
XLA Ops:
  0.6 50.8 %shard_map.75 = (bf16[32,1024]{1,0:T(8,128)(2,1)}, bf16[32,1024]{1,0:T(8,128)(2,1)}, f32[64,896]{1,0:T(8,128)}, f32[8,128]{1,0:T(8,128)}) custom-call(bf16[32,1024]{1,0:T(8,128)(2,1)} %vol_hbm.1, bf16[27,32,64]{2,1,0:T(8,128)(2,1)} %w_hbm.1, bf16[1,64]{1,0:T(2,128)(2,1)} %bitcast.2, bf16[32,1024]{1,0:T(8,128)(2,1)} %cot_hbm.1), custom_call_target="tpu_custom_call" | custom-call | tf_op jit(solution)/shard_map/pallas_call | solution.py:392
  51.4 2.0 %shard_map.76 = (bf16[32,1024]{1,0:T(8,128)(2,1)}, bf16[32,1024]{1,0:T(8,128)(2,1)}, f32[27,32,64]{2,1,0:T(8,128)}, f32[1,32]{1,0:T(1,128)}) custom-call(bf16[32,1024]{1,0:T(8,128)(2,1)} %get-tuple-element.12.out_in, bf16[32,1024]{1,0:T(8,128)(2,1)} %get-tuple-element.13.dgrad_in, f32[64,896]{1,0:T(8,128)} %get-tuple-element.14.wsum_in, ...), custom_call_target="tpu_custom_call" | custom-call | tf_op jit(solution)/shard_map/pallas_call | solution.py:439

commit v5 on v4

--- a/solution.py
+++ b/solution.py
@@ -74,7 +74,7 @@
 
     steps = [dx for dx in (1, 3, 2, 0) if dx < ny]
     col_steps = [(dy, dz) for dy in steps for dz in (1, 0)]
-    row_steps = [(dx, a, p) for dx in steps for a in (1, 0) for p in (1, 0)]
+    row_steps = [(dx, a, p) for a in (0, 1) for p in (0, 1) for dx in steps]
 
     def col_at(dy, dz):
         return 2 * around(ypos + dy) + flip(zpos, dz)
@@ -257,7 +257,8 @@
 
     for copy in g_copies:
         copy.wait_recv()
-    p_copies = []
+    early = list(copies)
+    p_copies = ([], [])
     lands = half_rows(CH * k + HALF * zpos)
     for o in (1, 0):
         h = flip(k, o)
@@ -270,7 +271,7 @@
         for dy, dz in col_steps:
             part = place(around(ypos + dy), dz)
             if dy or dz or o:
-                p_copies.append(
+                p_copies[o].append(
                     send(
                         wgp.at[h, part, :], wgrecv.at[dy, lands, :],
                         p_send.at[dy, dz, o], p_recv.at[dy, dz, o], sib if o else row, col_at(dy, dz),
@@ -279,38 +280,52 @@
             else:
                 wgrecv[0, lands, :] = wgp[h, part, :]
 
-    def spread(h):
+    def products(h):
         for p in range(2):
             z[p] = lax.dot_general(wg[h], g[p], TN, preferred_element_type=F32)
-        planes = []
-        for m in range(4):
-            total = jnp.zeros((CH, VOX), F32)
-            for b in range(3):
-                for c in range(3):
-                    part = None
-                    for p in range(2):
-                        if 0 <= m - p <= 2:
-                            start = VIEWS * (m - p) + CH * (3 * b + c)
-                            term = z[p, start : start + CH, :]
-                            part = term if part is None else part + term
-                    total = total + moved_view(part, y, x, 1 - b, 1 - c)
-            planes.append(total)
-        return planes
-
-    for m, total in enumerate(spread(1 - k)):
-        dsib[m] = total.astype(BF16)
-    d_copy = send(dsib, dsib_recv, d_send.at[0], d_recv.at[0], sib, col)
-    for m, total in enumerate(spread(k)):
-        dnear[m] = total
-    d_copy.wait_recv()
-    for m in range(4):
-        dnear[m] = dnear[m] + dsib_recv[m].astype(F32)
-    dfar[0] = dnear[0].astype(BF16)
-    dfar[1] = dnear[2 - zpos].astype(BF16)
-    dfar[2] = dnear[3].astype(BF16)
-    send(dfar.at[0], dfar_recv.at[1 + zpos], h_send.at[0], h_recv.at[1 + zpos], row, 2 * around(ypos - 1) + 1)
-    send(dfar.at[1], dfar_recv.at[0], h_send.at[1], h_recv.at[0], row, pair)
-    send(dfar.at[2], dfar_recv.at[1 + zpos], h_send.at[2], h_recv.at[1 + zpos], row, 2 * around(ypos + 1))
+
+    def spread(m):
+        total = jnp.zeros((CH, VOX), F32)
+        for b in range(3):
+            for c in range(3):
+                part = None
+                for p in range(2):
+                    if 0 <= m - p <= 2:
+                        start = VIEWS * (m - p) + CH * (3 * b + c)
+                        term = z[p, start : start + CH, :]
+                        part = term if part is None else part + term
+                total = total + moved_view(part, y, x, 1 - b, 1 - c)
+        return total
+
+    def send_far(slot, value, land, to_col):
+        dfar[slot] = value.astype(BF16)
+        send(dfar.at[slot], dfar_recv.at[land], h_send.at[slot], h_recv.at[land], row, to_col)
+
+    products(1 - k)
+    d_copies = {}
+    for m in (0, 3, 1, 2):
+        dsib[m] = spread(m).astype(BF16)
+        d_copies[m] = send(dsib.at[m], dsib_recv.at[m], d_send.at[m], d_recv.at[m], sib, col)
+    products(k)
+    for m in (0, 3, 1, 2):
+        total = spread(m)
+        d_copies[m].wait_recv()
+        total = total + dsib_recv[m].astype(F32)
+        if m == 0:
+            send_far(0, total, 1 + zpos, 2 * around(ypos - 1) + 1)
+        elif m == 3:
+            send_far(2, total, 1 + zpos, 2 * around(ypos + 1))
+        else:
+            dnear[m] = total
+    send_far(1, dnear[2 - zpos], 0, pair)
+
+    for copy in early:
+        copy.wait_send()
+    for sent, copy in later:
+
+        @pl.when(sent)
+        def _():
+            copy.wait_send()
 
     for copy in b_copies:
         copy.wait_recv()
@@ -321,6 +336,18 @@
     store_bias = pltpu.make_async_copy(bsum_v, bsum_hbm, store_sem.at[3])
     store_bias.start()
 
+    stores = [store_out, store_bias]
+    for o in (1, 0):
+        for copy in p_copies[o]:
+            copy.wait_recv()
+        part = other if o else mine
+        total = wgrecv[0, part, :].astype(F32)
+        for dy in range(1, ny):
+            total = total + wgrecv[dy, part, :].astype(F32)
+        wsum_v[part, :] = total * norm_factor
+        stores.append(pltpu.make_async_copy(wsum_v.at[part, :], wsum_hbm.at[part, :], store_sem.at[4 if o else 2]))
+        stores[-1].start()
+
     for i in range(3):
         arrived(dfar_recv.at[i], h_recv.at[i])
     cross_ok = jnp.where(zpos == 1, high_ok, low_ok)
@@ -330,24 +357,9 @@
     store_data = pltpu.make_async_copy(dgrad_v, dgrad_hbm, store_sem.at[1])
     store_data.start()
 
-    for copy in p_copies:
-        copy.wait_recv()
-    total = wgrecv[0].astype(F32)
-    for d in range(1, ny):
-        total = total + wgrecv[d].astype(F32)
-    wsum_v[...] = total * norm_factor
-    store_weights = pltpu.make_async_copy(wsum_v, wsum_hbm, store_sem.at[2])
-    store_weights.start()
-
-    for copy in copies:
+    for copy in copies[len(early) :]:
         copy.wait_send()
-    for sent, copy in later:
-
-        @pl.when(sent)
-        def _():
-            copy.wait_send()
-
-    for store in (store_out, store_data, store_weights, store_bias):
+    for store in (*stores, store_data):
         store.wait()
 
 
@@ -426,11 +438,11 @@
             pltpu.VMEM(plane, BF16),
             pltpu.VMEM((2 * CH, PADDED), F32),
             pltpu.VMEM((8, 128), F32),
-            dma((4,)), dma((4,)),
+            dma((4,)), dma((5,)),
             dma((3,)), dma((3,)), dma((4,)), dma((4,)),
             dma((ny, 2, 2)), dma((ny, 2, 2)),
             dma((nc, 2)), dma((nc, 2)), dma((nc, 2)), dma((nc, 2)), dma((nc,)), dma((nc,)),
-            dma((ny, 2, 2)), dma((ny, 2, 2)), dma((1,)), dma((1,)), dma((3,)), dma((3,)),
+            dma((ny, 2, 2)), dma((ny, 2, 2)), dma((4,)), dma((4,)), dma((3,)), dma((3,)),
         ],
         compiler_params=pltpu.CompilerParams(
             collective_id=0, has_side_effects=True, vmem_limit_bytes=VMEM_LIMIT

time: 53.6 us -> 53.4 us (level)
  no operation moved by 1% of the time
where the time goes in v5:
time: 53.4 us; the launch traced here: 53.2 us
  Pallas kernels  52.6 us (99%)
  between operations  0.64 us (1%)
    pallas_call x1, Pallas kernels, on_device(): pl.pallas_call(functools.partial(kernel, nc, 1.0 / math.sqrt(nc * VOX)),...  50.6 us
    pallas_call x1, Pallas kernels, on_device(): pl.pallas_call(finish, out_shape=(jax.ShapeDtypeStruct(plane, BF16), jax....  1.97 us

profile of v5, /device:TPU:1, one launch (start us, length us, event | category | flops | bytes accessed | tf_op | source)
XLA Modules:
  0.0 53.2 jit_solution(4121971826483255336)
XLA Ops:
  0.6 50.6 %shard_map.75 = (bf16[32,1024]{1,0:T(8,128)(2,1)}, bf16[32,1024]{1,0:T(8,128)(2,1)}, f32[64,896]{1,0:T(8,128)}, f32[8,128]{1,0:T(8,128)}) custom-call(bf16[32,1024]{1,0:T(8,128)(2,1)} %vol_hbm.1, bf16[27,32,64]{2,1,0:T(8,128)(2,1)} %w_hbm.1, bf16[1,64]{1,0:T(2,128)(2,1)} %bitcast.2, bf16[32,1024]{1,0:T(8,128)(2,1)} %cot_hbm.1), custom_call_target="tpu_custom_call" | custom-call | tf_op jit(solution)/shard_map/pallas_call | solution.py:404
  51.2 2.0 %shard_map.76 = (bf16[32,1024]{1,0:T(8,128)(2,1)}, bf16[32,1024]{1,0:T(8,128)(2,1)}, f32[27,32,64]{2,1,0:T(8,128)}, f32[1,32]{1,0:T(1,128)}) custom-call(bf16[32,1024]{1,0:T(8,128)(2,1)} %get-tuple-element.12.out_in, bf16[32,1024]{1,0:T(8,128)(2,1)} %get-tuple-element.13.dgrad_in, f32[64,896]{1,0:T(8,128)} %get-tuple-element.14.wsum_in, ...), custom_call_target="tpu_custom_call" | custom-call | tf_op jit(solution)/shard_map/pallas_call | solution.py:451

commit v6 on v5

--- a/solution.py
+++ b/solution.py
@@ -107,14 +107,15 @@
     mine, other = rows(CH * k), rows(CH * (1 - k))
     load_vol = pltpu.make_async_copy(vol_hbm, xin.at[1 + zpos, mine, :], load_sem.at[2])
     load_cot = pltpu.make_async_copy(cot_hbm, cot, load_sem.at[3])
-    for load in (load_w, load_bias, load_vol, load_cot):
-        load.start()
+    load_vol.start()
 
     barrier = pltpu.get_barrier_semaphore()
     peers = [(sib if o else row, col_at(dy, dz)) for dy, dz in col_steps for o in range(2) if dy or dz or o]
     peers += [(2 * pair_at(dx, a) + k, 2 * ypos + flip(zpos, p)) for dx, a, p in row_steps if dx or a or p]
     for peer in peers:
         pl.semaphore_signal(barrier, inc=1, device_id=peer, device_id_type=MESH)
+    for load in (load_w, load_bias, load_cot):
+        load.start()
 
     wpad[...] = jnp.zeros_like(wpad)
     bsend[...] = jnp.zeros_like(bsend)

time: 53.4 us -> 53.4 us (level)
  no operation moved by 1% of the time
where the time goes in v6:
time: 53.4 us; the launch traced here: 53.2 us
  Pallas kernels  52.6 us (99%)
  between operations  0.64 us (1%)
    pallas_call x1, Pallas kernels, on_device(): pl.pallas_call(functools.partial(kernel, nc, 1.0 / math.sqrt(nc * VOX)),...  50.6 us
    pallas_call x1, Pallas kernels, on_device(): pl.pallas_call(finish, out_shape=(jax.ShapeDtypeStruct(plane, BF16), jax....  1.97 us

profile of v6, /device:TPU:1, one launch (start us, length us, event | category | flops | bytes accessed | tf_op | source)
XLA Modules:
  0.0 53.2 jit_solution(676141009345289702)
XLA Ops:
  0.6 50.6 %shard_map.75 = (bf16[32,1024]{1,0:T(8,128)(2,1)}, bf16[32,1024]{1,0:T(8,128)(2,1)}, f32[64,896]{1,0:T(8,128)}, f32[8,128]{1,0:T(8,128)}) custom-call(bf16[32,1024]{1,0:T(8,128)(2,1)} %vol_hbm.1, bf16[27,32,64]{2,1,0:T(8,128)(2,1)} %w_hbm.1, bf16[1,64]{1,0:T(2,128)(2,1)} %bitcast.2, bf16[32,1024]{1,0:T(8,128)(2,1)} %cot_hbm.1), custom_call_target="tpu_custom_call" | custom-call | tf_op jit(solution)/shard_map/pallas_call | solution.py:405
  51.2 2.0 %shard_map.76 = (bf16[32,1024]{1,0:T(8,128)(2,1)}, bf16[32,1024]{1,0:T(8,128)(2,1)}, f32[27,32,64]{2,1,0:T(8,128)}, f32[1,32]{1,0:T(1,128)}) custom-call(bf16[32,1024]{1,0:T(8,128)(2,1)} %get-tuple-element.12.out_in, bf16[32,1024]{1,0:T(8,128)(2,1)} %get-tuple-element.13.dgrad_in, f32[64,896]{1,0:T(8,128)} %get-tuple-element.14.wsum_in, ...), custom_call_target="tpu_custom_call" | custom-call | tf_op jit(solution)/shard_map/pallas_call | solution.py:452
